TPU v7x, 512 devices: a whole 4x4x16 slice. The times are simulated.
512 devices in a mesh: pair: 32 (over z_lo, y), row: 4 (over z_hi, core), col: 4 (over x).
Axes of the slice: x: 4, y: 4, z: 16 (z_hi: 2, z_lo: 8; z = z_hi * 8 + z_lo), core: 2. Of those that a mesh axis runs over, the one named last changes fastest.
Arguments:
- intersection: float32 [32, 1280, 1280], P('pair', 'row', 'col'), as said below
- children: float32 [32, 1280, 1280], P('pair', 'row', 'col'), as said below
- band_start: int32 [10], replicated, may hold values from 0 to 2, as said below
- assignment: int32 [32, 5], replicated, may hold values from 0 to 1, as said below
Outputs:
- refined: float32 [32, 1280, 1280], P('pair', 'row', 'col')
- deviation: float32 [32, 1280, 1280], P('pair', 'row', 'col')
Inputs may be any that keep to these rules, and one draw needn't show every extreme that they name: band_start[i] <= i < band_start[i] + 8 for every block row i; the first block row starts at 0 and the last at 2. Every merge's row of assignment holds both values. `intersection`: each merge's matrix is symmetric with a positive diagonal that outweighs its off-diagonal part. `children`: each matrix is symmetric and is zero outside its upper left and lower right quadrants of order 1280 / 2.
All inputs are finite; a program needn't handle non-finite values.
Results may differ from a plain program's by a relative error of at most 0.0003.
Values sent between devices are 32-bit elements; how exact they have to be, the bound alone decides.
A program may use at most 64 MiB of HBM per device.

v0:
```python
import jax
import jax.numpy as jnp
from jax import lax
from jax.sharding import PartitionSpec as P

BLK = 128
BAND = 8


def passed_along(block, axis, distance):
    devices = range(lax.axis_size(axis))
    route = [((i - distance) % len(devices), i) for i in devices]
    return lax.ppermute(block, axis, route)


def skew_cols(tile, amount, levels):
    for level in range(levels):
        moved = passed_along(tile, "col", -(1 << level))
        tile = jnp.where(amount >> level & 1 == 1, moved, tile)
    return tile


def skew_rows(tile, amount, levels):
    for level in range(levels):
        moved = passed_along(tile, "row", -(1 << level))
        tile = jnp.where(amount >> level & 1 == 1, moved, tile)
    return tile


def cannon_product(left_skewed, right, col_index, count, levels):
    right_tile = skew_rows(right, col_index, levels)
    left_tile = left_skewed
    total = jnp.zeros((left_tile.shape[0], right_tile.shape[1]), jnp.float32)
    for step in range(count):
        total = total + jnp.dot(
            left_tile,
            right_tile,
            precision=lax.Precision.HIGHEST,
            preferred_element_type=jnp.float32,
        )
        if step + 1 < count:
            left_tile = passed_along(left_tile, "col", -1)
            right_tile = passed_along(right_tile, "row", -1)
    return total


def lookup(table, index):
    entries = jnp.arange(table.shape[0], dtype=jnp.int32)
    return jnp.sum(jnp.where(index[:, None] == entries[None, :], table[None, :], 0), axis=1)


def on_device(intersection, children, band_start, assignment):
    values = intersection[0]
    own = children[0]
    tile = values.shape[0]
    count = lax.axis_size("col")
    levels = count.bit_length() - 1
    row_index = lax.axis_index("row")
    col_index = lax.axis_index("col")
    group = lax.axis_index("pair")
    global_rows = row_index * tile + jnp.arange(tile, dtype=jnp.int32)
    global_cols = col_index * tile + jnp.arange(tile, dtype=jnp.int32)
    block_rows = global_rows // BLK
    block_cols = global_cols // BLK
    start_rows = lookup(band_start, block_rows)
    start_cols = lookup(band_start, block_cols)
    first = (block_cols[None, :] >= start_rows[:, None]) & (
        block_cols[None, :] < start_rows[:, None] + BAND
    )
    second = (block_rows[:, None] >= start_cols[None, :]) & (
        block_rows[:, None] < start_cols[None, :] + BAND
    )
    banded = jnp.where(first | second, values, jnp.float32(0.0))
    from_left = passed_along(own, "pair", 1)
    from_right = passed_along(own, "pair", -1)
    merges = jnp.arange(assignment.shape[0], dtype=jnp.int32)
    quarter = assignment.shape[1]
    group_row = jnp.sum(jnp.where((merges == group)[:, None], assignment, 0), axis=0)
    local_block = jnp.clip(block_rows - quarter, 0, quarter - 1)
    side_rows = lookup(group_row, local_block)
    half = count // 2
    lower = (row_index >= half) & (col_index >= half)
    supplied = jnp.where(side_rows[:, None] == 0, from_left, from_right)
    factor = jnp.where(lower, supplied, own)
    banded_skewed = skew_cols(banded, row_index, levels)
    factor_skewed = skew_cols(factor, row_index, levels)
    image = cannon_product(banded_skewed, factor, col_index, count, levels)
    congruence = cannon_product(factor_skewed, image, col_index, count, levels)
    correction = cannon_product(factor_skewed, congruence, col_index, count, levels)
    identity = jnp.where(global_rows[:, None] == global_cols[None, :], 1.0, 0.0).astype(jnp.float32)
    deviation = identity - congruence
    refined = 1.5 * factor - 0.5 * correction
    return (refined[None], deviation[None])


def solution(mesh):
    in_specs = (P("pair", "row", "col"), P("pair", "row", "col"), P(), P())
    out_specs = (P("pair", "row", "col"), P("pair", "row", "col"))
    return jax.shard_map(
        on_device, mesh=mesh, in_specs=in_specs, out_specs=out_specs, check_vma=False
    )
```

profile of v0, /device:TPU:7, one launch (start us, length us, event | category | flops | bytes accessed | tf_op | source)
XLA Modules:
  0.0 491.9 jit_solution(3000375121574261604)
XLA Ops:
  0.6 3.2 collective-permute-start
  3.8 14.0 %collective-permute-start.1 = (f32[320,320]{1,0:T(8,128)}, f32[320,320]{1,0:T(8,128)S(1)}, u32[]{:S(2)}, u32[]{:S(2)}) collective-permute-start(f32[320,320]{1,0:T(8,128)} %bitcast.35), channel_id=1, source_target_pairs={{16,0},{32,16},{48,32},{64,48},{80,64},{96,80},{112,96},{128,112},... | collective-permute-start | bytes 1228808 | tf_op jit(solution)/shard_map/ppermute | solution.py:13
  18.7 1.3 bitcast_select_fusion
  20.0 2.5 collective-permute-start.4
  23.5 3.7 collective-permute-done
  28.2 2.5 collective-permute-start.2
  30.7 3.7 collective-permute-start.6
  35.0 1.3 broadcast_select_fusion.6
  36.3 2.2 collective-permute-start.5
  38.5 9.3 %collective-permute-done.2 = f32[320,320]{1,0:T(8,128)S(1)} collective-permute-done((f32[320,320]{1,0:T(8,128)S(1)}, f32[320,320]{1,0:T(8,128)S(1)}, u32[]{:S(2)}, u32[]{:S(2)}) %collective-permute-start.2) | collective-permute-done | bytes 409632 | tf_op jit(solution)/shard_map/ppermute | solution.py:13
  47.8 16.9 %collective-permute-done.6 = f32[320,320]{1,0:T(8,128)S(1)} collective-permute-done((f32[320,320]{1,0:T(8,128)S(1)}, f32[320,320]{1,0:T(8,128)S(1)}, u32[]{:S(2)}, u32[]{:S(2)}) %collective-permute-start.6) | collective-permute-done | bytes 409632 | tf_op jit(solution)/shard_map/ppermute | solution.py:13
  64.8 8.1 %collective-permute-start.7 = (f32[320,320]{1,0:T(8,128)S(1)}, f32[320,320]{1,0:T(8,128)S(1)}, u32[]{:S(2)}, u32[]{:S(2)}) collective-permute-start(f32[320,320]{1,0:T(8,128)S(1)} %get-tuple-element.6), channel_id=1, source_target_pairs={{8,0},{12,4},{0,8},{4,12},{9,1},{13,5},{1,9},{5,13},{10,2},{14,6},... | collective-permute-start | bytes 1228808 | tf_op jit(solution)/shard_map/ppermute | solution.py:13
  73.0 2.7 collective-permute-start.8
  75.7 37.6 %collective-permute-done.7 = f32[320,320]{1,0:T(8,128)S(1)} collective-permute-done((f32[320,320]{1,0:T(8,128)S(1)}, f32[320,320]{1,0:T(8,128)S(1)}, u32[]{:S(2)}, u32[]{:S(2)}) %collective-permute-start.7) | collective-permute-done | bytes 409632 | tf_op jit(solution)/shard_map/ppermute | solution.py:13
  113.3 2.5 collective-permute-start.9
  115.8 2.4 collective-permute-start.10
  118.3 19.3 %collective-permute-done.9 = f32[320,320]{1,0:T(8,128)S(1)} collective-permute-done((f32[320,320]{1,0:T(8,128)S(1)}, f32[320,320]{1,0:T(8,128)S(1)}, u32[]{:S(2)}, u32[]{:S(2)}) %collective-permute-start.9) | collective-permute-done | bytes 409632 | tf_op jit(solution)/shard_map/ppermute | solution.py:13
  137.6 1.9 collective-permute-start.11
  139.5 2.1 collective-permute-start.12
  142.7 21.9 %collective-permute-done.11 = f32[320,320]{1,0:T(8,128)S(1)} collective-permute-done((f32[320,320]{1,0:T(8,128)S(1)}, f32[320,320]{1,0:T(8,128)S(1)}, u32[]{:S(2)}, u32[]{:S(2)}) %collective-permute-start.11) | collective-permute-done | bytes 409632 | tf_op jit(solution)/shard_map/ppermute | solution.py:13
  164.6 1.9 collective-permute-start.13
  167.7 1.1 convolution_add_fusion.7
  168.8 20.5 %collective-permute-done.13 = f32[320,320]{1,0:T(8,128)S(1)} collective-permute-done((f32[320,320]{1,0:T(8,128)S(1)}, f32[320,320]{1,0:T(8,128)S(1)}, u32[]{:S(2)}, u32[]{:S(2)}) %collective-permute-start.13) | collective-permute-done | bytes 409632 | tf_op jit(solution)/shard_map/ppermute | solution.py:13
  190.4 1.9 collective-permute-start.14
  192.3 2.7 collective-permute-start.3
  195.1 21.5 %collective-permute-done.14 = f32[320,320]{1,0:T(8,128)S(1)} collective-permute-done((f32[320,320]{1,0:T(8,128)S(1)}, f32[320,320]{1,0:T(8,128)S(1)}, u32[]{:S(2)}, u32[]{:S(2)}) %collective-permute-start.14) | collective-permute-done | bytes 409632 | tf_op jit(solution)/shard_map/ppermute | solution.py:13
  216.6 5.9 %collective-permute-start.15 = (f32[320,320]{1,0:T(8,128)S(1)}, f32[320,320]{1,0:T(8,128)S(1)}, u32[]{:S(2)}, u32[]{:S(2)}) collective-permute-start(f32[320,320]{1,0:T(8,128)S(1)} %broadcast_select_fusion.1), channel_id=1, source_target_pairs={{8,0},{12,4},{0,8},{4,12},{9,1},{13,5},{1,9},{5,13},{10,2},{14,6},... | collective-permute-start | bytes 1228808 | tf_op jit(solution)/shard_map/ppermute | solution.py:13
  222.6 2.1 collective-permute-start.16
  224.7 37.8 %collective-permute-done.15 = f32[320,320]{1,0:T(8,128)S(1)} collective-permute-done((f32[320,320]{1,0:T(8,128)S(1)}, f32[320,320]{1,0:T(8,128)S(1)}, u32[]{:S(2)}, u32[]{:S(2)}) %collective-permute-start.15) | collective-permute-done | bytes 409632 | tf_op jit(solution)/shard_map/ppermute | solution.py:13
  262.6 2.4 collective-permute-start.17
  265.0 2.1 collective-permute-start.18
  267.1 22.1 %collective-permute-done.17 = f32[320,320]{1,0:T(8,128)S(1)} collective-permute-done((f32[320,320]{1,0:T(8,128)S(1)}, f32[320,320]{1,0:T(8,128)S(1)}, u32[]{:S(2)}, u32[]{:S(2)}) %collective-permute-start.17) | collective-permute-done | bytes 409632 | tf_op jit(solution)/shard_map/ppermute | solution.py:13
  289.2 1.9 collective-permute-start.19
  291.1 2.5 collective-permute-start.20
  294.7 19.2 %collective-permute-done.19 = f32[320,320]{1,0:T(8,128)S(1)} collective-permute-done((f32[320,320]{1,0:T(8,128)S(1)}, f32[320,320]{1,0:T(8,128)S(1)}, u32[]{:S(2)}, u32[]{:S(2)}) %collective-permute-start.19) | collective-permute-done | bytes 409632 | tf_op jit(solution)/shard_map/ppermute | solution.py:13
  313.9 2.1 collective-permute-start.21
  318.2 22.8 %collective-permute-done.21 = f32[320,320]{1,0:T(8,128)S(1)} collective-permute-done((f32[320,320]{1,0:T(8,128)S(1)}, f32[320,320]{1,0:T(8,128)S(1)}, u32[]{:S(2)}, u32[]{:S(2)}) %collective-permute-start.21) | collective-permute-done | bytes 409632 | tf_op jit(solution)/shard_map/ppermute | solution.py:13
  342.0 1.9 collective-permute-start.22
  344.0 21.9 %collective-permute-done.22 = f32[320,320]{1,0:T(8,128)S(1)} collective-permute-done((f32[320,320]{1,0:T(8,128)S(1)}, f32[320,320]{1,0:T(8,128)S(1)}, u32[]{:S(2)}, u32[]{:S(2)}) %collective-permute-start.22) | collective-permute-done | bytes 409632 | tf_op jit(solution)/shard_map/ppermute | solution.py:13
  366.7 8.2 %collective-permute-start.23 = (f32[320,320]{1,0:T(8,128)S(1)}, f32[320,320]{1,0:T(8,128)S(1)}, u32[]{:S(2)}, u32[]{:S(2)}) collective-permute-start(f32[320,320]{1,0:T(8,128)S(1)} %get-tuple-element.5), channel_id=1, source_target_pairs={{8,0},{12,4},{0,8},{4,12},{9,1},{13,5},{1,9},{5,13},{10,2},{14,6},... | collective-permute-start | bytes 1228808 | tf_op jit(solution)/shard_map/ppermute | solution.py:13
  374.9 39.2 %collective-permute-done.23 = f32[320,320]{1,0:T(8,128)S(1)} collective-permute-done((f32[320,320]{1,0:T(8,128)S(1)}, f32[320,320]{1,0:T(8,128)S(1)}, u32[]{:S(2)}, u32[]{:S(2)}) %collective-permute-start.23) | collective-permute-done | bytes 409632 | tf_op jit(solution)/shard_map/ppermute | solution.py:13
  414.2 2.5 collective-permute-start.24
  416.7 21.8 %collective-permute-done.24 = f32[320,320]{1,0:T(8,128)S(1)} collective-permute-done((f32[320,320]{1,0:T(8,128)S(1)}, f32[320,320]{1,0:T(8,128)S(1)}, u32[]{:S(2)}, u32[]{:S(2)}) %collective-permute-start.24) | collective-permute-done | bytes 409632 | tf_op jit(solution)/shard_map/ppermute | solution.py:13
  438.5 1.9 collective-permute-start.25
  441.5 24.0 %collective-permute-done.25 = f32[320,320]{1,0:T(8,128)S(1)} collective-permute-done((f32[320,320]{1,0:T(8,128)S(1)}, f32[320,320]{1,0:T(8,128)S(1)}, u32[]{:S(2)}, u32[]{:S(2)}) %collective-permute-start.25) | collective-permute-done | bytes 409632 | tf_op jit(solution)/shard_map/ppermute | solution.py:13
  465.5 1.9 collective-permute-start.26
  469.6 20.4 %collective-permute-done.26 = f32[320,320]{1,0:T(8,128)S(1)} collective-permute-done((f32[320,320]{1,0:T(8,128)S(1)}, f32[320,320]{1,0:T(8,128)S(1)}, u32[]{:S(2)}, u32[]{:S(2)}) %collective-permute-start.26) | collective-permute-done | bytes 409632 | tf_op jit(solution)/shard_map/ppermute | solution.py:13
  490.0 1.9 fusion.2
  (47 shorter events, 15.5 us)
Async XLA Ops:
  0.6 26.5 %collective-permute-start = (f32[320,320]{1,0:T(8,128)}, f32[320,320]{1,0:T(8,128)S(1)}, u32[]{:S(2)}, u32[]{:S(2)}) collective-permute-start(f32[320,320]{1,0:T(8,128)} %bitcast.34), channel_id=1, source_target_pairs={{496,0},{0,16},{16,32},{32,48},{48,64},{64,80},{80,96},{96,112},{1... | collective-permute-start | bytes 1228808 | tf_op jit(solution)/shard_map/ppermute | solution.py:13
  3.8 24.2 %collective-permute-start.1 = (f32[320,320]{1,0:T(8,128)}, f32[320,320]{1,0:T(8,128)S(1)}, u32[]{:S(2)}, u32[]{:S(2)}) collective-permute-start(f32[320,320]{1,0:T(8,128)} %bitcast.35), channel_id=1, source_target_pairs={{16,0},{32,16},{48,32},{64,48},{80,64},{96,80},{112,96},{128,112},... | collective-permute-start | bytes 1228808 | tf_op jit(solution)/shard_map/ppermute | solution.py:13
  17.9 0.7 copy-start.3
  18.7 9.4 %copy-start.1 = (f32[1,320,320]{2,1,0:T(8,128)S(1)}, f32[1,320,320]{2,1,0:T(8,128)}, u32[]{:S(2)}) copy-start(f32[1,320,320]{2,1,0:T(8,128)} %param.5) | copy-start | bytes 1228804
  20.0 15.0 %collective-permute-start.4 = (f32[320,320]{1,0:T(8,128)S(1)}, f32[320,320]{1,0:T(8,128)}, u32[]{:S(2)}, u32[]{:S(2)}) collective-permute-start(f32[320,320]{1,0:T(8,128)S(1)} %bitcast_select_fusion), channel_id=1, source_target_pairs={{1,0},{2,1},{3,2},{0,3},{5,4},{6,5},{7,6},{4,7},{9,8},{10,9},{11,1... | collective-permute-start | bytes 1228808 | tf_op jit(solution)/shard_map/ppermute | solution.py:13
  22.5 0.7 copy-start.2
  23.4 11.6 %copy-start = (f32[1,320,320]{2,1,0:T(8,128)S(1)}, f32[1,320,320]{2,1,0:T(8,128)}, u32[]{:S(2)}) copy-start(f32[1,320,320]{2,1,0:T(8,128)} %param.4) | copy-start | bytes 1228804
  28.2 19.6 %collective-permute-start.2 = (f32[320,320]{1,0:T(8,128)S(1)}, f32[320,320]{1,0:T(8,128)S(1)}, u32[]{:S(2)}, u32[]{:S(2)}) collective-permute-start(f32[320,320]{1,0:T(8,128)S(1)} %select_select_fusion), channel_id=1, source_target_pairs={{1,0},{2,1},{3,2},{0,3},{5,4},{6,5},{7,6},{4,7},{9,8},{10,9},{11,1... | collective-permute-start | bytes 1228808 | tf_op jit(solution)/shard_map/ppermute | solution.py:13
  30.7 34.1 %collective-permute-start.6 = (f32[320,320]{1,0:T(8,128)S(1)}, f32[320,320]{1,0:T(8,128)S(1)}, u32[]{:S(2)}, u32[]{:S(2)}) collective-permute-start(f32[320,320]{1,0:T(8,128)S(1)} %select_select_fusion), channel_id=1, source_target_pairs={{4,0},{8,4},{12,8},{0,12},{5,1},{9,5},{13,9},{1,13},{6,2},{10,6},{... | collective-permute-start | bytes 1228808 | tf_op jit(solution)/shard_map/ppermute | solution.py:13
  36.3 36.6 %collective-permute-start.5 = (f32[320,320]{1,0:T(8,128)S(1)}, f32[320,320]{1,0:T(8,128)S(1)}, u32[]{:S(2)}, u32[]{:S(2)}) collective-permute-start(f32[320,320]{1,0:T(8,128)S(1)} %broadcast_select_fusion.6), channel_id=1, source_target_pairs={{2,0},{3,1},{0,2},{1,3},{6,4},{7,5},{4,6},{5,7},{10,8},{11,9},{8,1... | collective-permute-start | bytes 1228808 | tf_op jit(solution)/shard_map/ppermute | solution.py:13
  64.8 48.5 %collective-permute-start.7 = (f32[320,320]{1,0:T(8,128)S(1)}, f32[320,320]{1,0:T(8,128)S(1)}, u32[]{:S(2)}, u32[]{:S(2)}) collective-permute-start(f32[320,320]{1,0:T(8,128)S(1)} %get-tuple-element.6), channel_id=1, source_target_pairs={{8,0},{12,4},{0,8},{4,12},{9,1},{13,5},{1,9},{5,13},{10,2},{14,6},... | collective-permute-start | bytes 1228808 | tf_op jit(solution)/shard_map/ppermute | solution.py:13
  73.0 42.8 %collective-permute-start.8 = (f32[320,320]{1,0:T(8,128)S(1)}, f32[320,320]{1,0:T(8,128)S(1)}, u32[]{:S(2)}, u32[]{:S(2)}) collective-permute-start(f32[320,320]{1,0:T(8,128)S(1)} %broadcast_select_fusion.8), channel_id=1, source_target_pairs={{1,0},{2,1},{3,2},{0,3},{5,4},{6,5},{7,6},{4,7},{9,8},{10,9},{11,1... | collective-permute-start | bytes 1228808 | tf_op jit(solution)/shard_map/ppermute | solution.py:13
  113.3 24.3 %collective-permute-start.9 = (f32[320,320]{1,0:T(8,128)S(1)}, f32[320,320]{1,0:T(8,128)S(1)}, u32[]{:S(2)}, u32[]{:S(2)}) collective-permute-start(f32[320,320]{1,0:T(8,128)S(1)} %broadcast_select_fusion.5), channel_id=1, source_target_pairs={{4,0},{8,4},{12,8},{0,12},{5,1},{9,5},{13,9},{1,13},{6,2},{10,6},{... | collective-permute-start | bytes 1228808 | tf_op jit(solution)/shard_map/ppermute | solution.py:13
  115.8 23.7 %collective-permute-start.10 = (f32[320,320]{1,0:T(8,128)S(1)}, f32[320,320]{1,0:T(8,128)S(1)}, u32[]{:S(2)}, u32[]{:S(2)}) collective-permute-start(f32[320,320]{1,0:T(8,128)S(1)} %collective-permute-done.8), channel_id=1, source_target_pairs={{1,0},{2,1},{3,2},{0,3},{5,4},{6,5},{7,6},{4,7},{9,8},{10,9},{11,1... | collective-permute-start | bytes 1228808 | tf_op jit(solution)/shard_map/ppermute | solution.py:13
  137.6 27.1 %collective-permute-start.11 = (f32[320,320]{1,0:T(8,128)S(1)}, f32[320,320]{1,0:T(8,128)S(1)}, u32[]{:S(2)}, u32[]{:S(2)}) collective-permute-start(f32[320,320]{1,0:T(8,128)S(1)} %collective-permute-done.9), channel_id=1, source_target_pairs={{4,0},{8,4},{12,8},{0,12},{5,1},{9,5},{13,9},{1,13},{6,2},{10,6},{... | collective-permute-start | bytes 1228808 | tf_op jit(solution)/shard_map/ppermute | solution.py:13
  139.5 29.2 %collective-permute-start.12 = (f32[320,320]{1,0:T(8,128)S(1)}, f32[320,320]{1,0:T(8,128)S(1)}, u32[]{:S(2)}, u32[]{:S(2)}) collective-permute-start(f32[320,320]{1,0:T(8,128)S(1)} %collective-permute-done.10), channel_id=1, source_target_pairs={{1,0},{2,1},{3,2},{0,3},{5,4},{6,5},{7,6},{4,7},{9,8},{10,9},{11,1... | collective-permute-start | bytes 1228808 | tf_op jit(solution)/shard_map/ppermute | solution.py:13
  164.6 24.6 %collective-permute-start.13 = (f32[320,320]{1,0:T(8,128)S(1)}, f32[320,320]{1,0:T(8,128)S(1)}, u32[]{:S(2)}, u32[]{:S(2)}) collective-permute-start(f32[320,320]{1,0:T(8,128)S(1)} %collective-permute-done.11), channel_id=1, source_target_pairs={{4,0},{8,4},{12,8},{0,12},{5,1},{9,5},{13,9},{1,13},{6,2},{10,6},{... | collective-permute-start | bytes 1228808 | tf_op jit(solution)/shard_map/ppermute | solution.py:13
  190.4 26.2 %collective-permute-start.14 = (f32[320,320]{1,0:T(8,128)S(1)}, f32[320,320]{1,0:T(8,128)S(1)}, u32[]{:S(2)}, u32[]{:S(2)}) collective-permute-start(f32[320,320]{1,0:T(8,128)S(1)} %convolution_add_fusion.6), channel_id=1, source_target_pairs={{4,0},{8,4},{12,8},{0,12},{5,1},{9,5},{13,9},{1,13},{6,2},{10,6},{... | collective-permute-start | bytes 1228808 | tf_op jit(solution)/shard_map/ppermute | solution.py:13
  192.3 30.2 %collective-permute-start.3 = (f32[320,320]{1,0:T(8,128)S(1)}, f32[320,320]{1,0:T(8,128)S(1)}, u32[]{:S(2)}, u32[]{:S(2)}) collective-permute-start(f32[320,320]{1,0:T(8,128)S(1)} %get-tuple-element.7), channel_id=1, source_target_pairs={{2,0},{3,1},{0,2},{1,3},{6,4},{7,5},{4,6},{5,7},{10,8},{11,9},{8,1... | collective-permute-start | bytes 1228808 | tf_op jit(solution)/shard_map/ppermute | solution.py:13
  216.6 45.9 %collective-permute-start.15 = (f32[320,320]{1,0:T(8,128)S(1)}, f32[320,320]{1,0:T(8,128)S(1)}, u32[]{:S(2)}, u32[]{:S(2)}) collective-permute-start(f32[320,320]{1,0:T(8,128)S(1)} %broadcast_select_fusion.1), channel_id=1, source_target_pairs={{8,0},{12,4},{0,8},{4,12},{9,1},{13,5},{1,9},{5,13},{10,2},{14,6},... | collective-permute-start | bytes 1228808 | tf_op jit(solution)/shard_map/ppermute | solution.py:13
  222.6 42.4 %collective-permute-start.16 = (f32[320,320]{1,0:T(8,128)S(1)}, f32[320,320]{1,0:T(8,128)S(1)}, u32[]{:S(2)}, u32[]{:S(2)}) collective-permute-start(f32[320,320]{1,0:T(8,128)S(1)} %broadcast_select_fusion.9), channel_id=1, source_target_pairs={{1,0},{2,1},{3,2},{0,3},{5,4},{6,5},{7,6},{4,7},{9,8},{10,9},{11,1... | collective-permute-start | bytes 1228808 | tf_op jit(solution)/shard_map/ppermute | solution.py:13
  262.6 26.6 %collective-permute-start.17 = (f32[320,320]{1,0:T(8,128)S(1)}, f32[320,320]{1,0:T(8,128)S(1)}, u32[]{:S(2)}, u32[]{:S(2)}) collective-permute-start(f32[320,320]{1,0:T(8,128)S(1)} %broadcast_select_fusion.4), channel_id=1, source_target_pairs={{4,0},{8,4},{12,8},{0,12},{5,1},{9,5},{13,9},{1,13},{6,2},{10,6},{... | collective-permute-start | bytes 1228808 | tf_op jit(solution)/shard_map/ppermute | solution.py:13
  265.0 26.1 %collective-permute-start.18 = (f32[320,320]{1,0:T(8,128)S(1)}, f32[320,320]{1,0:T(8,128)S(1)}, u32[]{:S(2)}, u32[]{:S(2)}) collective-permute-start(f32[320,320]{1,0:T(8,128)S(1)} %collective-permute-done.16), channel_id=1, source_target_pairs={{1,0},{2,1},{3,2},{0,3},{5,4},{6,5},{7,6},{4,7},{9,8},{10,9},{11,1... | collective-permute-start | bytes 1228808 | tf_op jit(solution)/shard_map/ppermute | solution.py:13
  289.2 24.7 %collective-permute-start.19 = (f32[320,320]{1,0:T(8,128)S(1)}, f32[320,320]{1,0:T(8,128)S(1)}, u32[]{:S(2)}, u32[]{:S(2)}) collective-permute-start(f32[320,320]{1,0:T(8,128)S(1)} %collective-permute-done.17), channel_id=1, source_target_pairs={{4,0},{8,4},{12,8},{0,12},{5,1},{9,5},{13,9},{1,13},{6,2},{10,6},{... | collective-permute-start | bytes 1228808 | tf_op jit(solution)/shard_map/ppermute | solution.py:13
  291.1 27.0 %collective-permute-start.20 = (f32[320,320]{1,0:T(8,128)S(1)}, f32[320,320]{1,0:T(8,128)S(1)}, u32[]{:S(2)}, u32[]{:S(2)}) collective-permute-start(f32[320,320]{1,0:T(8,128)S(1)} %collective-permute-done.18), channel_id=1, source_target_pairs={{1,0},{2,1},{3,2},{0,3},{5,4},{6,5},{7,6},{4,7},{9,8},{10,9},{11,1... | collective-permute-start | bytes 1228808 | tf_op jit(solution)/shard_map/ppermute | solution.py:13
  313.9 27.0 %collective-permute-start.21 = (f32[320,320]{1,0:T(8,128)S(1)}, f32[320,320]{1,0:T(8,128)S(1)}, u32[]{:S(2)}, u32[]{:S(2)}) collective-permute-start(f32[320,320]{1,0:T(8,128)S(1)} %collective-permute-done.19), channel_id=1, source_target_pairs={{4,0},{8,4},{12,8},{0,12},{5,1},{9,5},{13,9},{1,13},{6,2},{10,6},{... | collective-permute-start | bytes 1228808 | tf_op jit(solution)/shard_map/ppermute | solution.py:13
  342.0 23.8 %collective-permute-start.22 = (f32[320,320]{1,0:T(8,128)S(1)}, f32[320,320]{1,0:T(8,128)S(1)}, u32[]{:S(2)}, u32[]{:S(2)}) collective-permute-start(f32[320,320]{1,0:T(8,128)S(1)} %convolution_add_fusion.3), channel_id=1, source_target_pairs={{4,0},{8,4},{12,8},{0,12},{5,1},{9,5},{13,9},{1,13},{6,2},{10,6},{... | collective-permute-start | bytes 1228808 | tf_op jit(solution)/shard_map/ppermute | solution.py:13
  366.7 47.4 %collective-permute-start.23 = (f32[320,320]{1,0:T(8,128)S(1)}, f32[320,320]{1,0:T(8,128)S(1)}, u32[]{:S(2)}, u32[]{:S(2)}) collective-permute-start(f32[320,320]{1,0:T(8,128)S(1)} %get-tuple-element.5), channel_id=1, source_target_pairs={{8,0},{12,4},{0,8},{4,12},{9,1},{13,5},{1,9},{5,13},{10,2},{14,6},... | collective-permute-start | bytes 1228808 | tf_op jit(solution)/shard_map/ppermute | solution.py:13
  414.2 24.3 %collective-permute-start.24 = (f32[320,320]{1,0:T(8,128)S(1)}, f32[320,320]{1,0:T(8,128)S(1)}, u32[]{:S(2)}, u32[]{:S(2)}) collective-permute-start(f32[320,320]{1,0:T(8,128)S(1)} %broadcast_select_fusion.3), channel_id=1, source_target_pairs={{4,0},{8,4},{12,8},{0,12},{5,1},{9,5},{13,9},{1,13},{6,2},{10,6},{... | collective-permute-start | bytes 1228808 | tf_op jit(solution)/shard_map/ppermute | solution.py:13
  438.5 27.1 %collective-permute-start.25 = (f32[320,320]{1,0:T(8,128)S(1)}, f32[320,320]{1,0:T(8,128)S(1)}, u32[]{:S(2)}, u32[]{:S(2)}) collective-permute-start(f32[320,320]{1,0:T(8,128)S(1)} %collective-permute-done.24), channel_id=1, source_target_pairs={{4,0},{8,4},{12,8},{0,12},{5,1},{9,5},{13,9},{1,13},{6,2},{10,6},{... | collective-permute-start | bytes 1228808 | tf_op jit(solution)/shard_map/ppermute | solution.py:13
  465.5 24.5 %collective-permute-start.26 = (f32[320,320]{1,0:T(8,128)S(1)}, f32[320,320]{1,0:T(8,128)S(1)}, u32[]{:S(2)}, u32[]{:S(2)}) collective-permute-start(f32[320,320]{1,0:T(8,128)S(1)} %collective-permute-done.25), channel_id=1, source_target_pairs={{4,0},{8,4},{12,8},{0,12},{5,1},{9,5},{13,9},{1,13},{6,2},{10,6},{... | collective-permute-start | bytes 1228808 | tf_op jit(solution)/shard_map/ppermute | solution.py:13
where the time goes:
time: 496 us; the launch traced here: 492 us
  waiting for transfers between devices  381 us (77%)
  starting transfers between devices  89.7 us (18%)
  matrix products  13.8 us (3%)
    ppermute x27, waiting for transfers between devices, passed_along(): return lax.ppermute(block, axis, route)  381 us
    ppermute x27, starting transfers between devices, passed_along(): return lax.ppermute(block, axis, route)  89.7 us
    dot_general x12, matrix products, cannon_product(): jnp.dot(left_tile, right_tile, precision=lax.Precision.HIGHEST, preferred...  13.8 us
  transfers between devices with their start and end apart: 27, of which 19 were waited for; matrix products, arithmetic and copies ran while one was open for 3% of the time, Pallas kernels for 0%

commit v1 on v0

v1 whole, which is shorter than its diff:
```python
import jax
import jax.numpy as jnp
from jax import lax
from jax.experimental import pallas as pl
from jax.experimental.pallas import tpu as pltpu
from jax.sharding import PartitionSpec as P

BLK = 128
BAND = 8
TILE = 320
HALF = 640
DIAG = 576
OFFD = 800
PART = 400
MESH = pl.DeviceIdType.MESH
F32 = jnp.float32
BF16 = jnp.bfloat16


def place():
    p = lax.axis_index("pair")
    row = lax.axis_index("row")
    x = lax.axis_index("col")
    h, c = row // 2, row % 2
    return p, h, c, x, (x + 2 * h) % 4


def device(p, h, c, u):
    return ((p + 32) % 32, 2 * h + c, (u + 2 * h) % 4)


def gather_kernel(assign, s, k, sq, lt, gd, go, raw, pkd, pko, zin, zout, send, recv):
    p, h, c, x, u = place()
    home = u < 2
    guest = u >= 2
    plane0 = h == 0
    plane1 = h == 1
    diag_home = home & (u == c)
    diag_guest = guest & (u - 2 == c)
    off_home = (u == 0) & (c == 1)
    relay = guest & (c == 1)
    landing = home & (c == 1)
    other = device(p, h, 1 - c, u)

    def copy(i, src, dst, to):
        return pltpu.make_async_remote_copy(
            src_ref=src, dst_ref=dst, send_sem=send.at[i], recv_sem=recv.at[i],
            device_id=to, device_id_type=MESH,
        )

    def on(cond, *acts):
        @pl.when(cond)
        def _():
            for act in acts:
                act()

    barrier = pltpu.get_barrier_semaphore()
    near = [device(p, h, c, (u + 1) % 4), device(p, h, c, (u + 2) % 4), device(p, h, c, (u + 3) % 4), other]
    far = [device(p, 1 - h, c, (u + 2) % 4)]
    for q in (p - 1, p + 1):
        far += [device(q, h, c, v) for v in range(4)]
    for d in far + near:
        pl.semaphore_signal(barrier, inc=1, device_id=d, device_id_type=MESH)

    own_s = 2 * c + u % 2
    far_s = 2 * c + 1 - u % 2
    first = jnp.where(home, 2 * c + u, 2 * c + 3 - u)
    second = jnp.where(home, 2 * c + 1 - u, 2 * c + u - 2)

    @pl.when(diag_home)
    def _():
        pkd[0:320] = k[:, 0:128]
        pkd[320:512] = k[128:320, 128:256]
        pkd[512:576, 0:64] = k[256:320, 256:320]
        pkd[512:576, 64:128] = jnp.zeros((64, 64), F32)

    @pl.when(off_home)
    def _():
        pko[0:320] = k[:, 0:128]
        pko[320:640] = k[:, 128:256]
        pko[640:800] = jnp.concatenate([k[0:160, 256:320], k[160:320, 256:320]], axis=1)

    sq[own_s] = s[...]

    @pl.when(home & plane0)
    def _():
        lt[first] = k[...]

    sx = copy(0, s, sq.at[own_s], device(p, h, c, u + 1 - 2 * (u % 2)))
    sc0 = copy(1, s, sq.at[own_s], other)
    sc1 = copy(2, sq.at[far_s], sq.at[far_s], other)
    yr = copy(3, k, raw.at[0], device(p + 1, h, c, u))
    yl = copy(4, k, raw.at[1], device(p - 1, h, c, u))
    hh = copy(5, lt.at[first], lt.at[first], device(p, h, c, 1 - u))
    hg = copy(6, lt.at[first], lt.at[first], device(p, h, c, 3 - u))
    gg = copy(7, lt.at[first], lt.at[first], device(p, h, c, 5 - u))
    ca = copy(8, lt.at[first], lt.at[first], other)
    cb = copy(9, lt.at[second], lt.at[second], other)
    zslot = jnp.where(plane0, 0, 2)
    zd = copy(10, pkd, gd.at[zslot], device(p, 1 - h, c, (u + 2) % 4))
    fr = copy(11, gd.at[2], gd.at[0], device(p + 1, h, c, u))
    fl = copy(12, gd.at[2], gd.at[1], device(p - 1, h, c, u))
    gs0 = copy(13, gd.at[0], gd.at[0], other)
    gs1 = copy(14, gd.at[1], gd.at[1], other)
    r0 = copy(15, pko.at[pl.ds(0, PART)], zin, device(p, h, c, 3))
    r1 = copy(16, pko.at[pl.ds(PART, PART)], zin, device(p, h, c, 2))
    zo = copy(17, zin, zout, device(p, 1 - h, c, (u + 2) % 4))
    part = 1 - u % 2
    begin = pl.multiple_of(part * PART, 8)
    ahead = jnp.where(plane0, p + 1, p)
    spread = [
        [copy(18 + part, zout, go.at[0, pl.ds(begin, PART)], device(ahead, h, c, 2)),
         copy(20 + part, zout, go.at[0, pl.ds(begin, PART)], device(ahead, h, c, 3))],
        [copy(22 + part, zout, go.at[1, pl.ds(begin, PART)], device(p - 1, h, c, 2)),
         copy(24 + part, zout, go.at[1, pl.ds(begin, PART)], device(p - 1, h, c, 3))],
    ]
    arrived = [
        [copy(18 + 2 * (u - 2) + i, zout, go.at[0, pl.ds(i * PART, PART)], other) for i in range(2)],
        [copy(22 + 2 * (u - 2) + i, zout, go.at[1, pl.ds(i * PART, PART)], other) for i in range(2)],
    ]
    os0 = copy(26, go.at[0], go.at[0], other)
    os1 = copy(27, go.at[1], go.at[1], other)

    pl.semaphore_wait(barrier, len(near) + len(far))

    on(off_home, r0.start, r1.start)
    on(diag_home, zd.start)
    on(home & plane1, yr.start, yl.start)
    on(home & plane0, hg.start, hh.start, ca.start)
    sx.start()
    sc0.start()

    on(relay & (u == 3), r0.wait_recv)
    on(relay & (u == 2), r1.wait_recv)
    on(relay, zo.start)

    @pl.when(home & plane1)
    def _():
        yr.wait_recv()
        yl.wait_recv()
        for j in range(5):
            rows = pl.ds(64 * j, 64)
            lt[first, rows] = jnp.where(assign[p, (5 * c + j) // 2] == 0, raw[0, rows], raw[1, rows])
        hg.start()
        hh.start()
        ca.start()

    sx.wait_recv()
    sc1.start()

    on(guest & plane0, hg.wait_recv, gg.start, ca.start, gg.wait_recv, cb.start)
    on(home & plane0, hh.wait_recv, cb.start)

    on(diag_guest & plane0, zd.wait_recv, fr.start, fl.start)
    on(landing, zo.wait_recv, spread[0][0].start, spread[0][1].start)
    on(landing & plane0, spread[1][0].start, spread[1][1].start)

    on(guest & plane1, hg.wait_recv, gg.start, ca.start, gg.wait_recv, cb.start)
    on(home & plane1, hh.wait_recv, cb.start)

    on(diag_guest & plane1, zd.wait_recv, gs0.start)
    on(diag_guest & plane0, fr.wait_recv, gs0.start, fl.wait_recv, gs1.start)
    on(relay, arrived[0][0].wait_recv, arrived[0][1].wait_recv, os0.start)
    on(relay & plane0, arrived[1][0].wait_recv, arrived[1][1].wait_recv, os1.start)

    sc0.wait_recv()
    sc1.wait_recv()
    ca.wait_recv()
    cb.wait_recv()
    on(guest & (u - 2 != c), gs0.wait_recv)
    on(guest & (u - 2 != c) & plane0, gs1.wait_recv)
    on(guest & (c == 0), os0.wait_recv)
    on(guest & (c == 0) & plane0, os1.wait_recv)

    sx.wait_send()
    sc0.wait_send()
    sc1.wait_send()
    ca.wait_send()
    cb.wait_send()
    on(home, hh.wait_send, hg.wait_send)
    on(guest, gg.wait_send)
    on(home & plane1, yr.wait_send, yl.wait_send)
    on(diag_home, zd.wait_send)
    on(off_home, r0.wait_send, r1.wait_send)
    on(relay, zo.wait_send, os0.wait_send)
    on(relay & plane0, os1.wait_send)
    on(diag_guest, gs0.wait_send)
    on(diag_guest & plane0, fr.wait_send, fl.wait_send, gs1.wait_send)
    on(landing, spread[0][0].wait_send, spread[0][1].wait_send)
    on(landing & plane0, spread[1][0].wait_send, spread[1][1].wait_send)


def split(v):
    hi = v.astype(BF16)
    return hi, (v - hi.astype(F32)).astype(BF16)


def dot3(ah, al, bh, bl):
    d = lambda a, b: jnp.dot(a, b, preferred_element_type=F32)
    return d(ah, bh) + (d(ah, bl) + d(al, bh))


def square(v):
    a, b, e = v[0:320], v[320:512], v[512:576, 0:64]
    r0 = jnp.concatenate([a[0:128], a[128:320].T], axis=1)
    r1 = jnp.concatenate([a[128:256], b[0:128], b[128:192].T], axis=1)
    r2 = jnp.concatenate([a[256:320], b[128:192], e], axis=1)
    return jnp.concatenate([r0, r1, r2], axis=0)


def oblong(v):
    e = v[640:800]
    return jnp.concatenate([v[0:320], v[320:640], jnp.concatenate([e[:, 0:64], e[:, 64:128]], axis=0)], axis=1)


def multiply_kernel(band, assign, k, sq, lt, gd, go, refined, deviation, lh, ll, sh, sl, th, tl, gh, gl, ch, cl):
    p, h, c, x, u = place()
    home = u < 2
    for r in range(2):
        rows = pl.ds(TILE * r, TILE)
        lh[rows], ll[rows] = split(jnp.concatenate([lt[2 * r], lt[2 * r + 1]], axis=1))
    hc = x // 2
    cols = lax.broadcasted_iota(jnp.int32, (1, HALF), 1) // BLK
    starts = jnp.zeros((1, HALF), jnp.int32)
    for j in range(5):
        starts = jnp.where(cols == j, band[5 * hc + j], starts)
    cols = cols + 5 * hc
    for i in range(10):
        r, local = i // 5, pl.ds(64 * (i % 5), 64)
        v = jnp.concatenate([sq[2 * r, local], sq[2 * r + 1, local]], axis=1)
        bi = 5 * h + i // 2
        st = band[bi]
        keep = ((cols >= st) & (cols < st + BAND)) | ((bi >= starts) & (bi < starts + BAND))
        rows = pl.ds(64 * i, 64)
        sh[rows], sl[rows] = split(jnp.where(keep, v, 0.0))

    @pl.loop(0, 5)
    def _(i):
        rows = pl.ds(pl.multiple_of(i * 128, 128), 128)
        th[rows], tl[rows] = split(dot3(lh[rows], ll[rows], sh[...], sl[...]))

    @pl.when(home)
    def _():
        for r in range(2):
            rows = pl.ds(TILE * r, TILE)
            gh[rows], gl[rows] = split(lt[2 * r + u])

    def put(r, v):
        rows = pl.ds(TILE * r, TILE)
        gh[rows], gl[rows] = split(v)

    def chosen(r, unpack, ref):
        a, b = unpack(ref[0]), unpack(ref[1])
        out = []
        for j in range(5):
            sel = assign[p, (5 * r + j) // 2] == 0
            out.append(jnp.where(sel, a[64 * j:64 * j + 64], b[64 * j:64 * j + 64]))
        return jnp.concatenate(out, axis=0)

    flipped = lambda v: oblong(v).T

    @pl.when((u == 2) & (h == 1))
    def _():
        put(0, square(gd[0]))
        put(1, oblong(go[0]))

    @pl.when((u == 3) & (h == 1))
    def _():
        put(0, flipped(go[0]))
        put(1, square(gd[0]))

    @pl.when((u == 2) & (h == 0))
    def _():
        put(0, chosen(0, square, gd))
        put(1, chosen(1, oblong, go))

    @pl.when((u == 3) & (h == 0))
    def _():
        put(0, chosen(0, flipped, go))
        put(1, chosen(1, square, gd))

    for r in range(2):
        rows = pl.ds(TILE * r, TILE)
        v = dot3(th[rows], tl[rows], gh[...], gl[...])
        ch[rows], cl[rows] = split(v)

        @pl.when(c == r)
        def _():
            eye = lax.broadcasted_iota(jnp.int32, (TILE, TILE), 0) == lax.broadcasted_iota(jnp.int32, (TILE, TILE), 1)
            deviation[...] = jnp.where(eye & (2 * h + c == x), 1.0, 0.0) - v

    rows = pl.ds(pl.multiple_of(TILE * c, TILE), TILE)
    corr = dot3(lh[rows], ll[rows], ch[...], cl[...])

    @pl.when(home)
    def _():
        refined[...] = 1.5 * lt[2 * c + u] - 0.5 * corr

    @pl.when(u >= 2)
    def _():
        refined[...] = 1.5 * k[...] - 0.5 * corr


def on_device(intersection, children, band_start, assignment):
    s, k = intersection[0], children[0]
    vm = pl.BlockSpec(memory_space=pltpu.VMEM)
    sm = pl.BlockSpec(memory_space=pltpu.SMEM)
    shape = lambda *d: jax.ShapeDtypeStruct(d, F32)
    sq, lt, gd, go = pl.pallas_call(
        gather_kernel,
        out_shape=(shape(4, TILE, TILE), shape(4, TILE, TILE), shape(3, DIAG, BLK), shape(2, OFFD, BLK)),
        in_specs=[sm, vm, vm],
        out_specs=(vm, vm, vm, vm),
        scratch_shapes=[
            pltpu.VMEM((2, TILE, TILE), F32),
            pltpu.VMEM((DIAG, BLK), F32),
            pltpu.VMEM((OFFD, BLK), F32),
            pltpu.VMEM((PART, BLK), F32),
            pltpu.VMEM((PART, BLK), F32),
            pltpu.SemaphoreType.DMA((28,)),
            pltpu.SemaphoreType.DMA((28,)),
        ],
        compiler_params=pltpu.CompilerParams(
            collective_id=0, has_side_effects=True, vmem_limit_bytes=32 << 20
        ),
        name="gather",
    )(assignment, s, k)
    half = lambda n: pltpu.VMEM((HALF, n), BF16)
    refined, deviation = pl.pallas_call(
        multiply_kernel,
        out_shape=(shape(TILE, TILE), shape(TILE, TILE)),
        in_specs=[sm, sm, vm, vm, vm, vm, vm],
        out_specs=(vm, vm),
        scratch_shapes=[half(HALF)] * 6 + [half(TILE)] * 4,
        compiler_params=pltpu.CompilerParams(vmem_limit_bytes=40 << 20),
        name="multiply",
    )(band_start, assignment, k, sq, lt, gd, go)
    return refined[None], deviation[None]


def solution(mesh):
    spec = P("pair", "row", "col")
    return jax.shard_map(
        on_device, mesh=mesh, in_specs=(spec, spec, P(), P()), out_specs=(spec, spec), check_vma=False
    )
```

time: 496 us -> 77.8 us (0.16)
  the two profiles are of different devices: /device:TPU:7 before, /device:TPU:507 now
where the time goes in v1:
time: 77.8 us; the launch traced here: 77.5 us
  Pallas kernels  72.3 us (93%)
  local copies, waits for them, and re-layouts  4.51 us (6%)
    pallas_call x1, Pallas kernels, on_device(): pl.pallas_call(gather_kernel, out_shape=(shape(4, TILE, TILE), shape(4, T...  63.4 us
    pallas_call x1, Pallas kernels, on_device(): pl.pallas_call(multiply_kernel, out_shape=(shape(TILE, TILE), shape(TILE,...  8.94 us
    unnamed x9, local copies, waits for them, and re-layouts  4.51 us

profile of v1, /device:TPU:507, one launch (start us, length us, event | category | flops | bytes accessed | tf_op | source)
XLA Modules:
  0.0 77.5 jit_solution(16156304018494573644)
XLA Ops:
  0.6 0.8 copy.7.assign
  1.4 0.0 copy-start
  1.4 1.0 %copy-done = f32[1,320,320]{2,1,0:T(8,128)S(1)} copy-done((f32[1,320,320]{2,1,0:T(8,128)S(1)}, f32[1,320,320]{2,1,0:T(8,128)}, u32[]{:S(2)}) %copy-start) | copy-done | bytes 409624
  2.4 0.0 copy-start.2
  2.4 1.0 %copy-done.2 = f32[1,320,320]{2,1,0:T(8,128)S(1)} copy-done((f32[1,320,320]{2,1,0:T(8,128)S(1)}, f32[1,320,320]{2,1,0:T(8,128)}, u32[]{:S(2)}) %copy-start.2) | copy-done | bytes 409624
  3.5 63.4 %gather.1 = (f32[4,320,320]{2,1,0:T(8,128)S(1)}, f32[4,320,320]{2,1,0:T(8,128)S(1)}, f32[3,576,128]{2,1,0:T(8,128)S(1)}, f32[2,800,128]{2,1,0:T(8,128)S(1)}) custom-call(s32[32,5]{1,0:T(8,128)S(1)} %copy.7.assign, f32[320,320]{1,0:T(8,128)S(1)} %bitcast.6, f32[320,320]{1,0:T(8,128)S(1)} %bitcast.4), custom_call_target="tpu_custom_call" | custom-call | tf_op jit(solution)/shard_map/gather/pallas_call | solution.py:309
  66.8 0.0 copy-start.1
  66.9 1.0 %copy-done.1 = f32[1,320,320]{2,1,0:T(8,128)S(1)} copy-done((f32[1,320,320]{2,1,0:T(8,128)S(1)}, f32[1,320,320]{2,1,0:T(8,128)}, u32[]{:S(2)}) %copy-start.1) | copy-done | bytes 409624
  67.9 0.0 copy-start.3
  67.9 0.7 copy-done.3
  68.5 8.9 %multiply.1 = (f32[320,320]{1,0:T(8,128)}, f32[320,320]{1,0:T(8,128)}) custom-call(s32[10]{0:T(128)S(1)} %copy-done.3, s32[32,5]{1,0:T(8,128)S(1)} %copy.7.assign, f32[320,320]{1,0:T(8,128)S(1)} %bitcast.5, f32[4,320,320]{2,1,0:T(8,128)S(1)} %get-tuple-element.8.sq, f32[4,320,320]{2,1,0:T(8,128)S(1)} %get-tuple-element.9.lt, ...), custom_call_target="tpu_custom_call" | custom-call | tf_op jit(solution)/shard_map/multiply/pallas_call | solution.py:329
Async XLA Ops:
  1.4 1.0 %copy-start = (f32[1,320,320]{2,1,0:T(8,128)S(1)}, f32[1,320,320]{2,1,0:T(8,128)}, u32[]{:S(2)}) copy-start(f32[1,320,320]{2,1,0:T(8,128)} %param.5) | copy-start | bytes 1228804
  2.4 1.0 %copy-start.2 = (f32[1,320,320]{2,1,0:T(8,128)S(1)}, f32[1,320,320]{2,1,0:T(8,128)}, u32[]{:S(2)}) copy-start(f32[1,320,320]{2,1,0:T(8,128)} %param.4) | copy-start | bytes 1228804
  66.8 1.0 %copy-start.1 = (f32[1,320,320]{2,1,0:T(8,128)S(1)}, f32[1,320,320]{2,1,0:T(8,128)}, u32[]{:S(2)}) copy-start(f32[1,320,320]{2,1,0:T(8,128)} %param.5) | copy-start | bytes 1228804
  67.9 0.7 copy-start.3

commit v2 on v1

v2 whole, which is shorter than its diff:
```python
import jax
import jax.numpy as jnp
from jax import lax
from jax.experimental import pallas as pl
from jax.experimental.pallas import tpu as pltpu
from jax.sharding import PartitionSpec as P

BLK = 128
BAND = 8
TILE = 320
HALF = 640
DIAG = 576
OFFD = 800
PART = 400
MESH = pl.DeviceIdType.MESH
F32 = jnp.float32
BF16 = jnp.bfloat16


def place():
    p = lax.axis_index("pair")
    row = lax.axis_index("row")
    x = lax.axis_index("col")
    h, c = row // 2, row % 2
    return p, h, c, x, (x + 2 * h) % 4


def device(p, h, c, u):
    return ((p + 32) % 32, 2 * h + c, (u + 2 * h) % 4)


def split(v):
    hi = v.astype(BF16)
    return hi, (v - hi.astype(F32)).astype(BF16)


def dot3(ah, al, bh, bl):
    d = lambda a, b: jnp.dot(a, b, preferred_element_type=F32)
    return d(ah, bh) + (d(ah, bl) + d(al, bh))


def square(v):
    a, b, e = v[0:320], v[320:512], v[512:576, 0:64]
    r0 = jnp.concatenate([a[0:128], a[128:320].T], axis=1)
    r1 = jnp.concatenate([a[128:256], b[0:128], b[128:192].T], axis=1)
    r2 = jnp.concatenate([a[256:320], b[128:192], e], axis=1)
    return jnp.concatenate([r0, r1, r2], axis=0)


def oblong(v):
    e = v[640:800]
    return jnp.concatenate([v[0:320], v[320:640], jnp.concatenate([e[:, 0:64], e[:, 64:128]], axis=0)], axis=1)


def flipped(v):
    return oblong(v).T


def gather_kernel(assign, s_hbm, k_hbm, sp, lp, gd, go, s, k, pko, zb, local, send, recv):
    p, h, c, x, u = place()
    home = u < 2
    guest = u >= 2
    plane0 = h == 0
    plane1 = h == 1
    high = x >= 2
    diag_home = home & (u == c)
    off_home = (u == 0) & (c == 1)
    relay = guest & (c == 1)
    landing = home & (c == 1)
    holds_diag = c == x % 2
    other = device(p, h, 1 - c, u)
    used = [0]

    def copy(src, dst, to, which=0, ways=1):
        i = used[0] + which
        used[0] += ways
        return pltpu.make_async_remote_copy(
            src_ref=src, dst_ref=dst, send_sem=send.at[i], recv_sem=recv.at[i],
            device_id=to, device_id_type=MESH,
        )

    def on(cond, *acts):
        @pl.when(cond)
        def _():
            for act in acts:
                act()

    def cut(ref, n, parts):
        return [ref.at[pl.ds(i * (n // parts), n // parts)] for i in range(parts)]

    def copies(src, dst, n, parts, to):
        return [copy(a, b, to) for a, b in zip(cut(src, n, parts), cut(dst, n, parts))]

    load_k = pltpu.make_async_copy(k_hbm, k, local.at[0])
    load_s = pltpu.make_async_copy(s_hbm, s, local.at[1])
    load_k.start()
    load_s.start()
    barrier = pltpu.get_barrier_semaphore()
    near = [device(p, h, c, (u + 1) % 4), device(p, h, c, (u + 2) % 4), device(p, h, c, (u + 3) % 4), other]
    near += [device(p, h, 1 - c, (u + 1) % 4), device(p, h, 1 - c, (u + 2) % 4), device(p, h, 1 - c, (u + 3) % 4)]
    far = [device(p, 1 - h, c, (u + 2) % 4)]
    for q in (p - 1, p + 1):
        far += [device(q, h, c, v) for v in range(4)]
        far += [device(q, h, 1 - c, v) for v in range(4)]
    for d in far + near:
        pl.semaphore_signal(barrier, inc=1, device_id=d, device_id_type=MESH)

    own_s = 2 * c + u % 2
    far_s = 2 * c + 1 - u % 2
    first = jnp.where(home, 2 * c + u, 2 * c + 3 - u)
    second = jnp.where(home, 2 * c + 1 - u, 2 * c + u - 2)

    def pack(ref, v):
        ref[0:320] = v[:, 0:128]
        ref[320:640] = v[:, 128:256]
        ref[640:800] = jnp.concatenate([v[0:160, 256:320], v[160:320, 256:320]], axis=1)

    load_k.wait()

    @pl.when(diag_home)
    def _():
        gd[2, 0:320] = k[:, 0:128]
        gd[2, 320:512] = k[128:320, 128:256]
        gd[2, 512:576, 0:64] = k[256:320, 256:320]
        gd[2, 512:576, 64:128] = jnp.zeros((64, 64), F32)

    @pl.when(off_home)
    def _():
        pack(pko, k)

    @pl.when(home & plane0)
    def _():
        pack(lp.at[first], k)

    load_s.wait()
    pack(sp.at[own_s], s)

    twin = device(p, 1 - h, c, (u + 2) % 4)
    r0 = copies(pko.at[pl.ds(0, PART)], zb, PART, 2, device(p, h, c, 3))
    r1 = copies(pko.at[pl.ds(PART, PART)], zb, PART, 2, device(p, h, c, 2))
    zo = copies(zb, zb, PART, 2, twin)
    zslot = jnp.where(plane0, 0, 2)
    zd = copies(gd.at[2], gd.at[zslot], DIAG, 2, twin)
    fr = copies(gd.at[2], gd.at[0], DIAG, 2, device(p + 1, h, c, u))
    fl = copies(gd.at[2], gd.at[1], DIAG, 2, device(p - 1, h, c, u))
    gs0 = copies(gd.at[0], gd.at[0], DIAG, 2, other)
    gs1 = copies(gd.at[1], gd.at[1], DIAG, 2, other)
    part = 1 - x % 2
    begin = pl.multiple_of(part * PART, 8)
    base = jnp.where(high, 0, 2)
    ahead = jnp.where(high, p, p + 1)
    spread0 = [[], []]
    spread1 = [[], []]
    arrived0 = []
    arrived1 = []
    for i in range(2):
        for slot, q, out, came in ((0, ahead, spread0, arrived0), (1, p - 1, spread1, arrived1)):
            target = (q + 32) % 32, 2 * h + 1 - i, base + i
            for j in range(2):
                at = used[0]
                dst = go.at[slot, pl.ds(begin + j * (PART // 2), PART // 2)]
                out[j].append(copy(zb.at[pl.ds(j * (PART // 2), PART // 2)], dst, target, part, 2))
                if i == 0:
                    came.append((at, j))
    used_go = used[0]
    span = 8

    def landed(at, j, n, slot):
        i = at + n + (x % 2) * span
        dst = go.at[slot, pl.ds(n * PART + j * (PART // 2), PART // 2)]
        return pltpu.make_async_remote_copy(
            src_ref=zb.at[pl.ds(0, PART // 2)], dst_ref=dst, send_sem=send.at[i], recv_sem=recv.at[i],
            device_id=other, device_id_type=MESH,
        )

    came0 = [landed(at, j, n, 0) for at, j in arrived0 for n in range(2)]
    came1 = [landed(at, j, n, 1) for at, j in arrived1 for n in range(2)]
    os0 = copy(go.at[0], go.at[0], other)
    os1 = copy(go.at[1], go.at[1], other)
    sx = copy(sp.at[own_s], sp.at[own_s], device(p, h, c, u + 1 - 2 * (u % 2)))
    sc0 = copy(sp.at[own_s], sp.at[own_s], other)
    sc1 = copy(sp.at[far_s], sp.at[far_s], other)
    hh = copy(lp.at[first], lp.at[first], device(p, h, c, 1 - u))
    hg = copies(lp.at[first], lp.at[first], OFFD, 2, device(p, h, c, 3 - u))
    gg = copies(lp.at[first], lp.at[first], OFFD, 2, device(p, h, c, 5 - u))
    ca = copy(lp.at[first], lp.at[first], other)
    cb = copy(lp.at[second], lp.at[second], other)

    starts = lambda cs: [d.start for d in cs]
    arrives = lambda cs: [d.wait_recv for d in cs]
    leaves = lambda cs: [d.wait_send for d in cs]

    pl.semaphore_wait(barrier, len(near) + len(far))

    on(off_home, r0[0].start, r1[0].start, r0[1].start, r1[1].start)
    on(diag_home, *starts(zd))
    on(diag_home & plane1, fr[0].start, fl[0].start, fr[1].start, fl[1].start)
    on(home & plane0, *starts(hg), hh.start, ca.start)
    sx.start()
    sc0.start()

    for j in range(2):
        on(relay & (u == 3), r0[j].wait_recv)
        on(relay & (u == 2), r1[j].wait_recv)
        on(relay, zo[j].start)
        on(relay & plane1, *starts(spread0[j]), *starts(spread1[j]))

    def settle(unpack, ref):
        a, b = unpack(ref[0]), unpack(ref[1])
        out = []
        for j in range(5):
            sel = assign[p, (5 * c + j) // 2] == 0
            out.append(jnp.where(sel, a[64 * j:64 * j + 64], b[64 * j:64 * j + 64]))
        pack(lp.at[first], jnp.concatenate(out, axis=0))

    def begin_left():
        for d in hg:
            d.start()
        hh.start()
        ca.start()

    @pl.when(diag_home & plane1)
    def _():
        for d in fr + fl:
            d.wait_recv()
        settle(square, gd)
        begin_left()

    @pl.when(home & (u != c) & plane1)
    def _():
        for d in came0 + came1:
            d.wait_recv()

        @pl.when(u == 0)
        def _():
            settle(oblong, go)

        @pl.when(u == 1)
        def _():
            settle(flipped, go)

        begin_left()

    sx.wait_recv()
    sc1.start()

    def left_side():
        for d, e in zip(hg, gg):
            d.wait_recv()
            e.start()
        ca.start()
        for d in gg:
            d.wait_recv()
        cb.start()

    on(guest & plane0, left_side)
    on(home & plane0, hh.wait_recv, cb.start)

    for j in range(2):
        on(guest & plane0 & holds_diag, zd[j].wait_recv, fr[j].start, fl[j].start)
        on(landing, zo[j].wait_recv, *starts(spread0[j]))
        on(landing & plane0, *starts(spread1[j]))

    on(guest & plane1, left_side)
    on(home & plane1, hh.wait_recv, cb.start)

    for j in range(2):
        on(guest & plane1 & holds_diag, zd[j].wait_recv, gs0[j].start)
        on(guest & plane0 & holds_diag, fr[j].wait_recv, gs0[j].start, fl[j].wait_recv, gs1[j].start)
    on(guest & ~holds_diag, *arrives(came0), os0.start)
    on(guest & plane0 & ~holds_diag, *arrives(came1), os1.start)

    sc0.wait_recv()
    sc1.wait_recv()
    ca.wait_recv()
    cb.wait_recv()
    on(guest & ~holds_diag, *arrives(gs0))
    on(guest & ~holds_diag & plane0, *arrives(gs1))
    on(guest & holds_diag, os0.wait_recv)
    on(guest & holds_diag & plane0, os1.wait_recv)

    for d in (sx, sc0, sc1, ca, cb):
        d.wait_send()
    on(home, hh.wait_send, *leaves(hg))
    on(guest, *leaves(gg))
    on(diag_home, *leaves(zd))
    on(high & holds_diag, *leaves(fr + fl))
    on(off_home, *leaves(r0 + r1))
    on(relay, *leaves(zo))
    on(guest & ~holds_diag, os0.wait_send)
    on(guest & ~holds_diag & plane0, os1.wait_send)
    on(guest & holds_diag, *leaves(gs0))
    on(guest & holds_diag & plane0, *leaves(gs1))
    on((c == 1) & (~high | plane1), *leaves(spread0[0] + spread0[1]))
    on((c == 1) & ~high, *leaves(spread1[0] + spread1[1]))


def multiply_kernel(band, assign, k, sp, lp, gd, go, refined, deviation, lh, ll, sh, sl, th, tl, gh, gl, ch, cl):
    p, h, c, x, u = place()
    home = u < 2
    for r in range(2):
        rows = pl.ds(TILE * r, TILE)
        lh[rows], ll[rows] = split(jnp.concatenate([oblong(lp[2 * r]), oblong(lp[2 * r + 1])], axis=1))
    hc = x // 2
    cols = lax.broadcasted_iota(jnp.int32, (1, HALF), 1) // BLK
    starts = jnp.zeros((1, HALF), jnp.int32)
    for j in range(5):
        starts = jnp.where(cols == j, band[5 * hc + j], starts)
    cols = cols + 5 * hc
    for i in range(10):
        r, local = i // 5, 64 * (i % 5)
        if i % 5 == 0:
            whole = jnp.concatenate([oblong(sp[2 * r]), oblong(sp[2 * r + 1])], axis=1)
        v = whole[local:local + 64]
        bi = 5 * h + i // 2
        st = band[bi]
        keep = ((cols >= st) & (cols < st + BAND)) | ((bi >= starts) & (bi < starts + BAND))
        rows = pl.ds(64 * i, 64)
        sh[rows], sl[rows] = split(jnp.where(keep, v, 0.0))

    @pl.loop(0, 5)
    def _(i):
        rows = pl.ds(pl.multiple_of(i * 128, 128), 128)
        th[rows], tl[rows] = split(dot3(lh[rows], ll[rows], sh[...], sl[...]))

    @pl.when(home)
    def _():
        for r in range(2):
            rows = pl.ds(TILE * r, TILE)
            gh[rows], gl[rows] = split(oblong(lp[2 * r + u]))

    def put(r, v):
        rows = pl.ds(TILE * r, TILE)
        gh[rows], gl[rows] = split(v)

    def chosen(r, unpack, ref):
        a, b = unpack(ref[0]), unpack(ref[1])
        out = []
        for j in range(5):
            sel = assign[p, (5 * r + j) // 2] == 0
            out.append(jnp.where(sel, a[64 * j:64 * j + 64], b[64 * j:64 * j + 64]))
        return jnp.concatenate(out, axis=0)

    @pl.when((u == 2) & (h == 1))
    def _():
        put(0, square(gd[0]))
        put(1, oblong(go[0]))

    @pl.when((u == 3) & (h == 1))
    def _():
        put(0, flipped(go[0]))
        put(1, square(gd[0]))

    @pl.when((u == 2) & (h == 0))
    def _():
        put(0, chosen(0, square, gd))
        put(1, chosen(1, oblong, go))

    @pl.when((u == 3) & (h == 0))
    def _():
        put(0, chosen(0, flipped, go))
        put(1, chosen(1, square, gd))

    for r in range(2):
        rows = pl.ds(TILE * r, TILE)
        v = dot3(th[rows], tl[rows], gh[...], gl[...])
        ch[rows], cl[rows] = split(v)

        @pl.when(c == r)
        def _():
            eye = lax.broadcasted_iota(jnp.int32, (TILE, TILE), 0) == lax.broadcasted_iota(jnp.int32, (TILE, TILE), 1)
            deviation[...] = jnp.where(eye & (2 * h + c == x), 1.0, 0.0) - v

    rows = pl.ds(pl.multiple_of(TILE * c, TILE), TILE)
    corr = dot3(lh[rows], ll[rows], ch[...], cl[...])

    @pl.when(home)
    def _():
        refined[...] = 1.5 * oblong(lp[2 * c + u]) - 0.5 * corr

    @pl.when(u >= 2)
    def _():
        refined[...] = 1.5 * k[...] - 0.5 * corr


def on_device(intersection, children, band_start, assignment):
    s, k = intersection[0], children[0]
    vm = pl.BlockSpec(memory_space=pltpu.VMEM)
    hb = pl.BlockSpec(memory_space=pl.ANY)
    sm = pl.BlockSpec(memory_space=pltpu.SMEM)
    shape = lambda *d: jax.ShapeDtypeStruct(d, F32)
    sp, lp, gd, go = pl.pallas_call(
        gather_kernel,
        out_shape=(shape(4, OFFD, BLK), shape(4, OFFD, BLK), shape(3, DIAG, BLK), shape(2, OFFD, BLK)),
        in_specs=[sm, hb, hb],
        out_specs=(vm, vm, vm, vm),
        scratch_shapes=[
            pltpu.VMEM((TILE, TILE), F32),
            pltpu.VMEM((TILE, TILE), F32),
            pltpu.VMEM((OFFD, BLK), F32),
            pltpu.VMEM((PART, BLK), F32),
            pltpu.SemaphoreType.DMA((2,)),
            pltpu.SemaphoreType.DMA((64,)),
            pltpu.SemaphoreType.DMA((64,)),
        ],
        compiler_params=pltpu.CompilerParams(
            collective_id=0, has_side_effects=True, vmem_limit_bytes=32 << 20
        ),
        name="gather",
    )(assignment, s, k)
    half = lambda n: pltpu.VMEM((HALF, n), BF16)
    refined, deviation = pl.pallas_call(
        multiply_kernel,
        out_shape=(shape(TILE, TILE), shape(TILE, TILE)),
        in_specs=[sm, sm, vm, vm, vm, vm, vm],
        out_specs=(vm, vm),
        scratch_shapes=[half(HALF)] * 6 + [half(TILE)] * 4,
        compiler_params=pltpu.CompilerParams(vmem_limit_bytes=40 << 20),
        name="multiply",
    )(band_start, assignment, k, sp, lp, gd, go)
    return refined[None], deviation[None]


def solution(mesh):
    spec = P("pair", "row", "col")
    return jax.shard_map(
        on_device, mesh=mesh, in_specs=(spec, spec, P(), P()), out_specs=(spec, spec), check_vma=False
    )
```

time: 77.8 us -> 68.8 us (0.88)
  the two profiles are of different devices: /device:TPU:507 before, /device:TPU:7 now
where the time goes in v2:
time: 68.8 us; the launch traced here: 68 us
  Pallas kernels  62.9 us (91%)
  local copies, waits for them, and re-layouts  4.51 us (7%)
    pallas_call x1, Pallas kernels, on_device(): pl.pallas_call(gather_kernel, out_shape=(shape(4, OFFD, BLK), shape(4, OF...  53.6 us
    pallas_call x1, Pallas kernels, on_device(): pl.pallas_call(multiply_kernel, out_shape=(shape(TILE, TILE), shape(TILE,...  9.23 us
    unnamed x9, local copies, waits for them, and re-layouts  4.51 us

profile of v2, /device:TPU:7, one launch (start us, length us, event | category | flops | bytes accessed | tf_op | source)
XLA Modules:
  0.0 68.0 jit_solution(1261115550932754481)
XLA Ops:
  0.6 0.8 %copy.7.assign = s32[32,5]{1,0:T(8,128)S(1)} copy(s32[32,5]{0,1:T(8,128)} %param.7) | data formatting | bytes 1280 | tf_op args[3]
  1.4 0.0 copy-start
  1.4 1.0 %copy-done = f32[1,320,320]{2,1,0:T(8,128)S(1)} copy-done((f32[1,320,320]{2,1,0:T(8,128)S(1)}, f32[1,320,320]{2,1,0:T(8,128)}, u32[]{:S(2)}) %copy-start) | copy-done | bytes 409624
  2.4 0.0 copy-start.2
  2.4 1.0 %copy-done.2 = f32[1,320,320]{2,1,0:T(8,128)S(1)} copy-done((f32[1,320,320]{2,1,0:T(8,128)S(1)}, f32[1,320,320]{2,1,0:T(8,128)}, u32[]{:S(2)}) %copy-start.2) | copy-done | bytes 409624
  3.5 53.6 %gather.1 = (f32[4,800,128]{2,1,0:T(8,128)S(1)}, f32[4,800,128]{2,1,0:T(8,128)S(1)}, f32[3,576,128]{2,1,0:T(8,128)S(1)}, f32[2,800,128]{2,1,0:T(8,128)S(1)}) custom-call(s32[32,5]{1,0:T(8,128)S(1)} %copy.7.assign, f32[320,320]{1,0:T(8,128)S(1)} %bitcast.6, f32[320,320]{1,0:T(8,128)S(1)} %bitcast.4), custom_call_target="tpu_custom_call" | custom-call | tf_op jit(solution)/shard_map/gather/pallas_call | solution.py:392
  57.1 0.0 copy-start.1
  57.1 1.0 %copy-done.1 = f32[1,320,320]{2,1,0:T(8,128)S(1)} copy-done((f32[1,320,320]{2,1,0:T(8,128)S(1)}, f32[1,320,320]{2,1,0:T(8,128)}, u32[]{:S(2)}) %copy-start.1) | copy-done | bytes 409624
  58.1 0.0 copy-start.3
  58.1 0.7 copy-done.3
  58.8 9.2 %multiply.1 = (f32[320,320]{1,0:T(8,128)}, f32[320,320]{1,0:T(8,128)}) custom-call(s32[10]{0:T(128)S(1)} %copy-done.3, s32[32,5]{1,0:T(8,128)S(1)} %copy.7.assign, f32[320,320]{1,0:T(8,128)S(1)} %bitcast.5, f32[4,800,128]{2,1,0:T(8,128)S(1)} %get-tuple-element.8.sp, f32[4,800,128]{2,1,0:T(8,128)S(1)} %get-tuple-element.9.lp, ...), custom_call_target="tpu_custom_call" | custom-call | tf_op jit(solution)/shard_map/multiply/pallas_call | solution.py:412
Async XLA Ops:
  1.4 1.0 %copy-start = (f32[1,320,320]{2,1,0:T(8,128)S(1)}, f32[1,320,320]{2,1,0:T(8,128)}, u32[]{:S(2)}) copy-start(f32[1,320,320]{2,1,0:T(8,128)} %param.5) | copy-start | bytes 1228804
  2.4 1.0 %copy-start.2 = (f32[1,320,320]{2,1,0:T(8,128)S(1)}, f32[1,320,320]{2,1,0:T(8,128)}, u32[]{:S(2)}) copy-start(f32[1,320,320]{2,1,0:T(8,128)} %param.4) | copy-start | bytes 1228804
  57.1 1.0 %copy-start.1 = (f32[1,320,320]{2,1,0:T(8,128)S(1)}, f32[1,320,320]{2,1,0:T(8,128)}, u32[]{:S(2)}) copy-start(f32[1,320,320]{2,1,0:T(8,128)} %param.5) | copy-start | bytes 1228804
  58.1 0.7 copy-start.3

commit v3 on v2

v3 whole, which is shorter than its diff:
```python
import jax
import jax.numpy as jnp
from jax import lax
from jax.experimental import pallas as pl
from jax.experimental.pallas import tpu as pltpu
from jax.sharding import PartitionSpec as P

BLK = 128
BAND = 8
TILE = 320
HALF = 640
DIAG = 576
OFFD = 800
PART = 400
MERGES = 32
MESH = pl.DeviceIdType.MESH
F32 = jnp.float32
BF16 = jnp.bfloat16


def place():
    p = lax.axis_index("pair")
    row = lax.axis_index("row")
    x = lax.axis_index("col")
    h, c = row // 2, row % 2
    return p, h, c, x, (x + 2 * h) % 4


def device(p, h, c, u):
    return ((p + MERGES) % MERGES, 2 * h + c, (u + 2 * h) % 4)


def split(v):
    hi = v.astype(BF16)
    return hi, (v - hi.astype(F32)).astype(BF16)


def dot3(ah, al, bh, bl):
    d = lambda a, b: jnp.dot(a, b, preferred_element_type=F32)
    return d(ah, bh) + (d(ah, bl) + d(al, bh))


def pack(ref, v):
    ref[0:320] = v[:, 0:128]
    ref[320:640] = v[:, 128:256]
    ref[640:800] = jnp.concatenate([v[0:160, 256:320], v[160:320, 256:320]], axis=1)


def oblong(v):
    e = v[640:800]
    return jnp.concatenate([v[0:320], v[320:640], jnp.concatenate([e[:, 0:64], e[:, 64:128]], axis=0)], axis=1)


def flipped(v):
    return oblong(v).T


def square(v):
    a, b, e = v[0:320], v[320:512], v[512:576, 0:64]
    r0 = jnp.concatenate([a[0:128], a[128:320].T], axis=1)
    r1 = jnp.concatenate([a[128:256], b[0:128], b[128:192].T], axis=1)
    r2 = jnp.concatenate([a[256:320], b[128:192], e], axis=1)
    return jnp.concatenate([r0, r1, r2], axis=0)


def refine_kernel(
    band, assign, s_hbm, k_hbm, refined, deviation,
    sp, lp, gd, go, s, k, ko, zb, lh, ll, sh, sl, th, tl, wh, wl, gh, gl, yh, yl_, ch, cl, local, send, recv,
):
    p, h, c, x, u = place()
    home = u < 2
    guest = u >= 2
    plane0 = h == 0
    plane1 = h == 1
    high = x >= 2
    diag_home = home & (u == c)
    off_home = home & (u != c)
    relay = guest & (c == 1)
    landing = home & (c == 1)
    holds_diag = c == x % 2
    first_off = jnp.where(home, u, 3 - u) != c
    other = device(p, h, 1 - c, u)
    used = [0]

    def copy(src, dst, to, which=0, ways=1, came=None):
        i = used[0] + which
        used[0] += ways
        return pltpu.make_async_remote_copy(
            src_ref=src, dst_ref=dst, send_sem=send.at[i], recv_sem=recv.at[i if came is None else came],
            device_id=to, device_id_type=MESH,
        )

    def on(cond, *acts):
        @pl.when(cond)
        def _():
            for act in acts:
                act()

    def cut(ref, n, parts):
        return [ref.at[pl.ds(i * (n // parts), n // parts)] for i in range(parts)]

    def copies(src, dst, n, parts, to):
        return [copy(a, b, to) for a, b in zip(cut(src, n, parts), cut(dst, n, parts))]

    load_k = pltpu.make_async_copy(k_hbm, k, local.at[0])
    load_s = pltpu.make_async_copy(s_hbm, s, local.at[1])
    load_k.start()
    load_s.start()
    barrier = pltpu.get_barrier_semaphore()
    friends = [device(p, 1 - h, c, (u + 2) % 4)]
    for q in (p - 1, p + 1):
        friends += [device(q, h, b, v) for v in range(4) for b in range(2)]
    friends += [device(p, h, b, (u + v) % 4) for v in range(4) for b in (c, 1 - c) if v or b is not c]
    for d in friends:
        pl.semaphore_signal(barrier, inc=1, device_id=d, device_id_type=MESH)
    last = (p == MERGES - 1) & plane1
    zeroth = (p == 0) & plane1
    seam = last | zeroth | ((p == 0) & plane0) | ((p == MERGES - 1) & plane0)

    @pl.when(seam)
    def _():
        for b in range(2):
            for v in range(4):
                d = (MERGES - 1 - p, 2 * (1 - h) + b, v)
                pl.semaphore_signal(barrier, inc=1, device_id=d, device_id_type=MESH)

    own_s = 2 * c + u % 2
    far_s = 2 * c + 1 - u % 2
    first = jnp.where(home, 2 * c + u, 2 * c + 3 - u)
    second = jnp.where(home, 2 * c + 1 - u, 2 * c + u - 2)

    load_k.wait()

    @pl.when(diag_home)
    def _():
        gd[2, 0:320] = k[:, 0:128]
        gd[2, 320:512] = k[128:320, 128:256]
        gd[2, 512:576, 0:64] = k[256:320, 256:320]
        gd[2, 512:576, 64:128] = jnp.zeros((64, 64), F32)

    @pl.when(off_home)
    def _():
        pack(ko, k)

    @pl.when(home & plane0)
    def _():
        pack(lp.at[first], k)

    load_s.wait()
    pack(sp.at[own_s], s)

    NZ, NR, NL = 4, 5, 5
    step = PART // NR
    twin = device(p, 1 - h, c, (u + 2) % 4)
    r0 = copies(ko.at[pl.ds(0, PART)], zb, PART, NR, device(p, h, c, 3))
    r1 = copies(ko.at[pl.ds(PART, PART)], zb, PART, NR, device(p, h, c, 2))
    zo = copies(zb, zb, PART, NR, twin)
    zd = copies(gd.at[2], gd.at[jnp.where(plane0, 0, 2)], DIAG, NZ, twin)
    at_r = used[0]
    fr = copies(gd.at[2], gd.at[0], DIAG, NZ, device(p + 1, h, c, u))
    at_l = used[0]
    fl = copies(gd.at[2], gd.at[1], DIAG, NZ, device(p - 1, h, c, u))
    yr = copies(ko, go.at[0], OFFD, NL, device(p + 1, h, c, u))
    yl = copies(ko, go.at[1], OFFD, NL, device(p - 1, h, c, u))
    gs0 = copies(gd.at[0], gd.at[0], DIAG, NZ, other)
    gs1 = copies(gd.at[1], gd.at[1], DIAG, NZ, other)
    part = 1 - x % 2
    begin = pl.multiple_of(part * PART, 8)
    base = jnp.where(high, 0, 2)
    ahead = jnp.where(high, p, p + 1)
    spread = [[[] for _ in range(NR)] for _ in range(2)]
    across = [[[] for _ in range(NR)] for _ in range(2)]
    at_go = used[0]
    for i in range(2):
        for slot, q in ((0, ahead), (1, p - 1)):
            for j in range(NR):
                at = used[0]
                src, dst = zb.at[pl.ds(j * step, step)], go.at[slot, pl.ds(begin + j * step, step)]
                spread[slot][j].append(copy(src, dst, ((q + MERGES) % MERGES, 2 * h + 1 - i, base + i), part, 2))
                to = (MERGES - 1 - p, 1 - i, 2 + i)
                across[slot][j].append(copy(src, dst, to, came=at + part))

    def landed(slot, n, j):
        i = at_go + (slot * NR + j) * 3 + n + (x % 2) * (2 * NR * 3)
        return pltpu.make_async_remote_copy(
            src_ref=zb.at[pl.ds(0, step)], dst_ref=go.at[slot, pl.ds(n * PART + j * step, step)],
            send_sem=send.at[i], recv_sem=recv.at[i], device_id=other, device_id_type=MESH,
        )

    came = [[[landed(slot, n, j) for j in range(NR)] for n in range(2)] for slot in range(2)]
    sr = [copy(a, b, (MERGES - 1 - p, c, x), came=at_r + i) for i, (a, b) in enumerate(zip(cut(gd.at[2], DIAG, NZ), cut(gd.at[0], DIAG, NZ)))]
    sw = [copy(a, b, (MERGES - 1 - p, c, x), came=at_l + i) for i, (a, b) in enumerate(zip(cut(gd.at[2], DIAG, NZ), cut(gd.at[1], DIAG, NZ)))]
    os0 = copies(go.at[0], go.at[0], OFFD, 2, other)
    os1 = copies(go.at[1], go.at[1], OFFD, 2, other)
    sx = copy(sp.at[own_s], sp.at[own_s], device(p, h, c, u + 1 - 2 * (u % 2)))
    sc0 = copy(sp.at[own_s], sp.at[own_s], other)
    sc1 = copy(sp.at[far_s], sp.at[far_s], other)
    hh = copy(lp.at[first], lp.at[first], device(p, h, c, 1 - u))
    hg = copies(lp.at[first], lp.at[first], OFFD, NL, device(p, h, c, 3 - u))
    gg = copies(lp.at[first], lp.at[first], OFFD, NL, device(p, h, c, 5 - u))
    ca = copy(lp.at[first], lp.at[first], other)
    cb = copy(lp.at[second], lp.at[second], other)

    starts = lambda cs: [d.start for d in cs]
    arrives = lambda cs: [d.wait_recv for d in cs]
    leaves = lambda cs: [d.wait_send for d in cs]
    both = lambda a, b: [d for pair in zip(a, b) for d in pair]
    flat = lambda a: [d for b in a for d in b]

    pl.semaphore_wait(barrier, len(friends) + 8 * seam.astype(jnp.int32))

    on(off_home & (u == 0), *starts(both(r0, r1)))
    on(diag_home, *starts(zd))
    on(diag_home & plane1, *starts(both(fr, fl)))
    on(diag_home & last, *starts(sr))
    on(diag_home & zeroth, *starts(sw))
    on(off_home & plane1, *starts(both(yr, yl)))
    on(home & plane0, *starts(hg), ca.start)
    on(diag_home & plane0, hh.start)
    on(guest | diag_home, sx.start)
    sc0.start()

    for j in range(NR):
        on(relay & (u == 3), r0[j].wait_recv)
        on(relay & (u == 2), r1[j].wait_recv)
        on(relay, zo[j].start)
        on(relay & last, *starts(across[0][j]))
        on(relay & zeroth, *starts(across[1][j]))

    def pick(row, a, b):
        return jnp.where(assign[(5 * c + row // 64) // 2, p] == 0, a, b)

    @pl.when(diag_home & plane1)
    def _():
        for d in fr + fl:
            d.wait_recv()
        a, b = square(gd[0]), square(gd[1])
        pack(lp.at[first], jnp.concatenate([pick(i, a[i:i + 64], b[i:i + 64]) for i in range(0, 320, 64)], axis=0))
        for d in hg + [hh, ca]:
            d.start()

    @pl.when(off_home & plane1)
    def _():
        edges = ((0, 64, 128, 160), (160, 192, 256, 320))
        for j in range(NL):
            yr[j].wait_recv()
            yl[j].wait_recv()
            if j < 4:
                e = edges[j % 2]
                for lo, hi in zip(e, e[1:]):
                    at = pl.ds(320 * (j // 2) + lo, hi - lo)
                    lp[first, at] = pick(lo, go[0, at], go[1, at])
            else:
                for lo, hi in ((0, 32), (32, 64), (64, 96), (96, 128), (128, 160)):
                    at = pl.ds(640 + lo, hi - lo)
                    a, b = go[0, at], go[1, at]
                    lp[first, at] = jnp.concatenate(
                        [pick(lo, a[:, 0:64], b[:, 0:64]), pick(160 + lo, a[:, 64:128], b[:, 64:128])], axis=1
                    )
            hg[j].start()
        hh.start()
        ca.start()

    on(guest | off_home, sx.wait_recv, sc1.start)

    for j in range(NL):
        on(guest, hg[j].wait_recv)
        on(guest & (plane1 | ~first_off), gg[j].start)
    on(guest, ca.start)
    on(guest & plane0 & first_off, *arrives(gg), cb.start)
    on(off_home & plane0, hh.wait_recv, cb.start)

    for j in range(NZ):
        on(guest & plane0 & holds_diag, zd[j].wait_recv)
        on(guest & plane0 & holds_diag & (p < MERGES - 1), fr[j].start)
        on(guest & plane0 & holds_diag & (p > 0), fl[j].start)
        on(guest & plane1 & holds_diag, zd[j].wait_recv, gs0[j].start)
    for j in range(NR):
        on(landing, zo[j].wait_recv)
        on(landing & (plane1 | (p < MERGES - 1)), *starts(spread[0][j]))
        on(landing & plane0 & (p > 0), *starts(spread[1][j]))
    on(home & plane1, hh.wait_recv, cb.start)

    sc0.wait_recv()
    on(guest | diag_home, sc1.wait_recv)

    @pl.when(home)
    def _():
        pack(sp.at[1 + u], flipped(sp[2 - u]))

    hc = x // 2
    cols = lax.broadcasted_iota(jnp.int32, (1, HALF), 1) // BLK
    begins = jnp.zeros((1, HALF), jnp.int32)
    for j in range(5):
        begins = jnp.where(cols == j, band[5 * hc + j], begins)
    cols = cols + 5 * hc
    for r in range(2):
        whole = jnp.concatenate([oblong(sp[2 * r]), oblong(sp[2 * r + 1])], axis=1)
        for i in range(5):
            bi = 5 * h + (5 * r + i) // 2
            st = band[bi]
            keep = ((cols >= st) & (cols < st + BAND)) | ((bi >= begins) & (bi < begins + BAND))
            rows = pl.ds(TILE * r + 64 * i, 64)
            sh[rows], sl[rows] = split(jnp.where(keep, whole[64 * i:64 * i + 64], 0.0))

    def left():
        @pl.when(plane0)
        def _():
            @pl.when((u == 0) | (u == 3))
            def _():
                pack(lp.at[1], flipped(lp[2]))

            @pl.when((u == 1) | (u == 2))
            def _():
                pack(lp.at[2], flipped(lp[1]))

        for r in range(2):
            rows = pl.ds(TILE * r, TILE)
            lh[rows], ll[rows] = split(jnp.concatenate([oblong(lp[2 * r]), oblong(lp[2 * r + 1])], axis=1))

    def right(r, v):
        rows = pl.ds(TILE * r, TILE)
        gh[rows], gl[rows] = split(v)

    def store_deviation(v):
        eye = lax.broadcasted_iota(jnp.int32, (TILE, TILE), 0) == lax.broadcasted_iota(jnp.int32, (TILE, TILE), 1)
        deviation[...] = jnp.where(eye & (2 * h + c == x), 1.0, 0.0) - v

    own_rows = pl.ds(pl.multiple_of(TILE * c, 64), TILE)

    def values_times_right():
        @pl.loop(0, 5)
        def _(i):
            rows = pl.ds(pl.multiple_of(i * 128, 128), 128)
            yh[rows], yl_[rows] = split(dot3(sh[rows], sl[rows], gh[...], gl[...]))

    def left_times_that():
        for r in range(2):
            rows = pl.ds(TILE * r, TILE)
            v = dot3(lh[rows], ll[rows], yh[...], yl_[...])
            ch[rows], cl[rows] = split(v)

            @pl.when(c == r)
            def _():
                store_deviation(v)

        return dot3(lh[own_rows], ll[own_rows], ch[...], cl[...])

    @pl.when(guest & plane0)
    def _():
        ca.wait_recv()

        @pl.when(~first_off)
        def _():
            cb.wait_recv()

        left()

        @pl.loop(0, 5)
        def _(i):
            rows = pl.ds(pl.multiple_of(i * 128, 128), 128)
            th[rows], tl[rows] = split(dot3(lh[rows], ll[rows], sh[...], sl[...]))

        wh[0:320], wl[0:320] = th[own_rows], tl[own_rows]
        for i in range(2):
            rows = pl.ds(pl.multiple_of(TILE * c + 160 * i, 32), 160)
            at = pl.ds(320 + 160 * i, 160)
            wh[at], wl[at] = split(dot3(lh[rows], ll[rows], th[...], tl[...]))

    on(guest & plane0 & holds_diag, *[a for j in range(NZ) for a in (fr[j].wait_recv, gs0[j].start, fl[j].wait_recv, gs1[j].start)])
    for n in range(2):
        on(guest & ~holds_diag, *arrives(came[0][n]), os0[n].start)
        on(guest & plane0 & ~holds_diag, *arrives(came[1][n]), os1[n].start)
    on(guest & ~holds_diag, *arrives(gs0))
    on(guest & ~holds_diag & plane0, *arrives(gs1))
    on(guest & holds_diag, *arrives(os0))
    on(guest & holds_diag & plane0, *arrives(os1))

    def chosen(r, unpack, ref):
        a, b = unpack(ref[0]), unpack(ref[1])
        out = []
        for j in range(5):
            sel = assign[(5 * r + j) // 2, p] == 0
            out.append(jnp.where(sel, a[64 * j:64 * j + 64], b[64 * j:64 * j + 64]))
        return jnp.concatenate(out, axis=0)

    @pl.when(guest & plane0)
    def _():
        @pl.when(u == 2)
        def _():
            right(0, chosen(0, square, gd))
            right(1, chosen(1, oblong, go))

        @pl.when(u == 3)
        def _():
            right(0, chosen(0, flipped, go))
            right(1, chosen(1, square, gd))

        store_deviation(dot3(wh[0:320], wl[0:320], gh[...], gl[...]))
        refined[...] = 1.5 * k[...] - 0.5 * dot3(wh[320:640], wl[320:640], gh[...], gl[...])

    @pl.when(guest & plane1)
    def _():
        @pl.when(u == 2)
        def _():
            right(0, square(gd[0]))
            right(1, oblong(go[0]))

        @pl.when(u == 3)
        def _():
            right(0, flipped(go[0]))
            right(1, square(gd[0]))

        values_times_right()
        for d in gg:
            d.wait_recv()
        cb.start()
        ca.wait_recv()
        cb.wait_recv()
        left()
        refined[...] = 1.5 * k[...] - 0.5 * left_times_that()

    @pl.when(home)
    def _():
        ca.wait_recv()

        @pl.when(plane1 | (u == c))
        def _():
            cb.wait_recv()

        left()
        for r in range(2):
            right(r, oblong(lp[2 * r + u]))
        values_times_right()
        refined[...] = 1.5 * oblong(lp[2 * c + u]) - 0.5 * left_times_that()

    sc0.wait_send()
    ca.wait_send()
    on(guest | diag_home, sx.wait_send)
    on(guest | off_home, sc1.wait_send)
    on(plane1 | first_off, cb.wait_send)
    on(home & (plane1 | ~first_off), hh.wait_send)
    on(home, *leaves(hg))
    on(guest & (plane1 | ~first_off), *leaves(gg))
    on(diag_home, *leaves(zd))
    on(diag_home & plane1, *leaves(fr + fl))
    on(diag_home & last, *leaves(sr))
    on(diag_home & zeroth, *leaves(sw))
    on(guest & plane0 & holds_diag & (p < MERGES - 1), *leaves(fr))
    on(guest & plane0 & holds_diag & (p > 0), *leaves(fl))
    on(off_home & plane1, *leaves(yr + yl))
    on(off_home & (u == 0), *leaves(r0 + r1))
    on(relay, *leaves(zo))
    on(relay & last, *leaves(flat(across[0])))
    on(relay & zeroth, *leaves(flat(across[1])))
    on(landing & (plane1 | (p < MERGES - 1)), *leaves(flat(spread[0])))
    on(landing & plane0 & (p > 0), *leaves(flat(spread[1])))
    on(guest & ~holds_diag, *leaves(os0))
    on(guest & ~holds_diag & plane0, *leaves(os1))
    on(guest & holds_diag, *leaves(gs0))
    on(guest & holds_diag & plane0, *leaves(gs1))


def on_device(intersection, children, band_start, assignment):
    s, k = intersection[0], children[0]
    vm = pl.BlockSpec(memory_space=pltpu.VMEM)
    sm = pl.BlockSpec(memory_space=pltpu.SMEM)
    hb = pl.BlockSpec(memory_space=pltpu.HBM)
    shape = jax.ShapeDtypeStruct((TILE, TILE), F32)
    vmem = lambda *d: pltpu.VMEM(d, F32)
    half = lambda n: pltpu.VMEM((HALF, n), BF16)
    refined, deviation = pl.pallas_call(
        refine_kernel,
        out_shape=(shape, shape),
        in_specs=[sm, sm, hb, hb],
        out_specs=(vm, vm),
        scratch_shapes=[
            vmem(4, OFFD, BLK), vmem(4, OFFD, BLK), vmem(3, DIAG, BLK), vmem(2, OFFD, BLK),
            vmem(TILE, TILE), vmem(TILE, TILE), vmem(OFFD, BLK), vmem(PART, BLK),
        ]
        + [half(HALF)] * 8
        + [half(TILE)] * 6
        + [
            pltpu.SemaphoreType.DMA((2,)),
            pltpu.SemaphoreType.DMA((160,)),
            pltpu.SemaphoreType.DMA((160,)),
        ],
        compiler_params=pltpu.CompilerParams(
            collective_id=0, has_side_effects=True, vmem_limit_bytes=48 << 20
        ),
        name="refine",
    )(band_start, assignment.T, s, k)
    return refined[None], deviation[None]


def solution(mesh):
    spec = P("pair", "row", "col")
    return jax.shard_map(
        on_device, mesh=mesh, in_specs=(spec, spec, P(), P()), out_specs=(spec, spec), check_vma=False
    )
```

time: 68.8 us -> 62.2 us (0.904)
  the two profiles are of different devices: /device:TPU:7 before, /device:TPU:258 now
where the time goes in v3:
time: 62.2 us; the launch traced here: 61.9 us
  Pallas kernels  57 us (92%)
  local copies, waits for them, and re-layouts  4.29 us (7%)
  between operations  0.66 us (1%)
    pallas_call x1, Pallas kernels, on_device(): pl.pallas_call(refine_kernel, out_shape=(shape, shape), in_specs=[sm, sm,...  57 us
    unnamed x10, local copies, waits for them, and re-layouts  4.29 us

profile of v3, /device:TPU:258, one launch (start us, length us, event | category | flops | bytes accessed | tf_op | source)
XLA Modules:
  0.0 61.9 jit_solution(6250802700302315086)
XLA Ops:
  0.6 0.0 copy-start.2
  0.6 0.0 copy-start.3
  0.7 0.7 %copy-done.2 = s32[32,5]{0,1:T(8,128)S(1)} copy-done((s32[32,5]{0,1:T(8,128)S(1)}, s32[32,5]{0,1:T(8,128)}, u32[]{:S(2)}) %copy-start.2) | copy-done | bytes 664
  1.3 0.0 copy-done.3
  1.3 0.0 copy-start
  1.3 1.0 %copy-done = f32[1,320,320]{2,1,0:T(8,128)S(1)} copy-done((f32[1,320,320]{2,1,0:T(8,128)S(1)}, f32[1,320,320]{2,1,0:T(8,128)}, u32[]{:S(2)}) %copy-start) | copy-done | bytes 409624
  2.4 0.0 copy-start.1
  2.4 1.0 %copy-done.1 = f32[1,320,320]{2,1,0:T(8,128)S(1)} copy-done((f32[1,320,320]{2,1,0:T(8,128)S(1)}, f32[1,320,320]{2,1,0:T(8,128)}, u32[]{:S(2)}) %copy-start.1) | copy-done | bytes 409624
  3.4 57.0 %refine.1 = (f32[320,320]{1,0:T(8,128)S(1)}, f32[320,320]{1,0:T(8,128)S(1)}) custom-call(s32[10]{0:T(128)S(1)} %copy-done.3, s32[5,32]{1,0:T(8,128)S(1)} %bitcast.9, f32[320,320]{1,0:T(8,128)S(1)} %bitcast.5, f32[320,320]{1,0:T(8,128)S(1)} %bitcast.6), custom_call_target="tpu_custom_call" | custom-call | tf_op jit(solution)/shard_map/refine/pallas_call | solution.py:472
  60.4 0.8 %copy.8 = f32[1,320,320]{2,1,0:T(8,128)} copy(f32[1,320,320]{2,1,0:T(8,128)S(1)} %bitcast.8) | data formatting | bytes 819200
  61.2 0.8 %copy.9 = f32[1,320,320]{2,1,0:T(8,128)} copy(f32[1,320,320]{2,1,0:T(8,128)S(1)} %bitcast.7) | data formatting | bytes 819200
Async XLA Ops:
  0.6 0.7 %copy-start.2 = (s32[32,5]{0,1:T(8,128)S(1)}, s32[32,5]{0,1:T(8,128)}, u32[]{:S(2)}) copy-start(s32[32,5]{0,1:T(8,128)} %param.7) | copy-start | bytes 1924
  0.6 0.7 %copy-start.3 = (s32[10]{0:T(128)S(1)}, s32[10]{0:T(128)}, u32[]{:S(2)}) copy-start(s32[10]{0:T(128)} %band.1) | copy-start | bytes 124
  1.3 1.0 %copy-start = (f32[1,320,320]{2,1,0:T(8,128)S(1)}, f32[1,320,320]{2,1,0:T(8,128)}, u32[]{:S(2)}) copy-start(f32[1,320,320]{2,1,0:T(8,128)} %param.4) | copy-start | bytes 1228804
  2.4 1.0 %copy-start.1 = (f32[1,320,320]{2,1,0:T(8,128)S(1)}, f32[1,320,320]{2,1,0:T(8,128)}, u32[]{:S(2)}) copy-start(f32[1,320,320]{2,1,0:T(8,128)} %param.5) | copy-start | bytes 1228804

commit v4 on v3

--- a/solution.py
+++ b/solution.py
@@ -65,7 +65,7 @@
 
 def refine_kernel(
     band, assign, s_hbm, k_hbm, refined, deviation,
-    sp, lp, gd, go, s, k, ko, zb, lh, ll, sh, sl, th, tl, wh, wl, gh, gl, yh, yl_, ch, cl, local, send, recv,
+    sp, lp, gd, go, s, k, ko, zb, zn, zs, lh, ll, sh, sl, th, tl, wh, wl, gh, gl, yh, yl_, ch, cl, local, send, recv,
 ):
     p, h, c, x, u = place()
     home = u < 2
@@ -167,37 +167,41 @@
     part = 1 - x % 2
     begin = pl.multiple_of(part * PART, 8)
     base = jnp.where(high, 0, 2)
-    ahead = jnp.where(high, p, p + 1)
-    spread = [[[] for _ in range(NR)] for _ in range(2)]
-    across = [[[] for _ in range(NR)] for _ in range(2)]
+    at_n = used[0]
+    nr = copies(zb, zn.at[0], PART, NR, device(p + 1, h, c, u))
+    nl = copies(zb, zn.at[1], PART, NR, device(p - 1, h, c, u))
+    seam_r = [copy(a, b, (MERGES - 1 - p, c, x), came=at_n + i) for i, (a, b) in enumerate(zip(cut(zb, PART, NR), cut(zn.at[0], PART, NR)))]
+    seam_l = [copy(a, b, (MERGES - 1 - p, c, x), came=at_n + NR + i) for i, (a, b) in enumerate(zip(cut(zb, PART, NR), cut(zn.at[1], PART, NR)))]
+    spread = [[] for _ in range(NR)]
+    chosen_spread = [[] for _ in range(NR)]
     at_go = used[0]
     for i in range(2):
-        for slot, q in ((0, ahead), (1, p - 1)):
-            for j in range(NR):
-                at = used[0]
-                src, dst = zb.at[pl.ds(j * step, step)], go.at[slot, pl.ds(begin + j * step, step)]
-                spread[slot][j].append(copy(src, dst, ((q + MERGES) % MERGES, 2 * h + 1 - i, base + i), part, 2))
-                to = (MERGES - 1 - p, 1 - i, 2 + i)
-                across[slot][j].append(copy(src, dst, to, came=at + part))
-
-    def landed(slot, n, j):
-        i = at_go + (slot * NR + j) * 3 + n + (x % 2) * (2 * NR * 3)
+        for j in range(NR):
+            at = used[0]
+            rows, dst = pl.ds(j * step, step), go.at[0, pl.ds(begin + j * step, step)]
+            to = (p, 2 * h + 1 - i, base + i)
+            spread[j].append(copy(zb.at[rows], dst, to, part, 2))
+            used[0] = at
+            chosen_spread[j].append(copy(zs.at[i, rows], dst, to, part, 2))
+
+    def landed(n, j):
+        i = at_go + j * 2 + n + (x % 2) * (2 * NR)
         return pltpu.make_async_remote_copy(
-            src_ref=zb.at[pl.ds(0, step)], dst_ref=go.at[slot, pl.ds(n * PART + j * step, step)],
+            src_ref=zb.at[pl.ds(0, step)], dst_ref=go.at[0, pl.ds(n * PART + j * step, step)],
             send_sem=send.at[i], recv_sem=recv.at[i], device_id=other, device_id_type=MESH,
         )
 
-    came = [[[landed(slot, n, j) for j in range(NR)] for n in range(2)] for slot in range(2)]
+    came = [[landed(n, j) for j in range(NR)] for n in range(2)]
     sr = [copy(a, b, (MERGES - 1 - p, c, x), came=at_r + i) for i, (a, b) in enumerate(zip(cut(gd.at[2], DIAG, NZ), cut(gd.at[0], DIAG, NZ)))]
     sw = [copy(a, b, (MERGES - 1 - p, c, x), came=at_l + i) for i, (a, b) in enumerate(zip(cut(gd.at[2], DIAG, NZ), cut(gd.at[1], DIAG, NZ)))]
     os0 = copies(go.at[0], go.at[0], OFFD, 2, other)
-    os1 = copies(go.at[1], go.at[1], OFFD, 2, other)
     sx = copy(sp.at[own_s], sp.at[own_s], device(p, h, c, u + 1 - 2 * (u % 2)))
     sc0 = copy(sp.at[own_s], sp.at[own_s], other)
     sc1 = copy(sp.at[far_s], sp.at[far_s], other)
-    hh = copy(lp.at[first], lp.at[first], device(p, h, c, 1 - u))
+    hh = copies(lp.at[first], lp.at[first], OFFD, NL, device(p, h, c, 1 - u))
     hg = copies(lp.at[first], lp.at[first], OFFD, NL, device(p, h, c, 3 - u))
-    gg = copies(lp.at[first], lp.at[first], OFFD, NL, device(p, h, c, 5 - u))
+    gg = copies(lp.at[first], lp.at[first], OFFD, NL, device(p, h, c, 5 - u))[:3]
+    hf = copies(lp.at[second], lp.at[second], OFFD, NL, device(p, h, c, 3 - u))[3:]
     ca = copy(lp.at[first], lp.at[first], other)
     cb = copy(lp.at[second], lp.at[second], other)
 
@@ -210,22 +214,24 @@
     pl.semaphore_wait(barrier, len(friends) + 8 * seam.astype(jnp.int32))
 
     on(off_home & (u == 0), *starts(both(r0, r1)))
-    on(diag_home, *starts(zd))
+    y = p % 4
     on(diag_home & plane1, *starts(both(fr, fl)))
     on(diag_home & last, *starts(sr))
     on(diag_home & zeroth, *starts(sw))
+    on(diag_home, *starts(zd))
     on(off_home & plane1, *starts(both(yr, yl)))
     on(home & plane0, *starts(hg), ca.start)
-    on(diag_home & plane0, hh.start)
+    on(diag_home & plane0, *starts(hh))
     on(guest | diag_home, sx.start)
     sc0.start()
 
+    late = plane0 & ((y == 0) | (y == 3))
     for j in range(NR):
         on(relay & (u == 3), r0[j].wait_recv)
         on(relay & (u == 2), r1[j].wait_recv)
-        on(relay, zo[j].start)
-        on(relay & last, *starts(across[0][j]))
-        on(relay & zeroth, *starts(across[1][j]))
+        on(relay & ~late, zo[j].start)
+        on(relay & last, seam_r[j].start)
+        on(relay & zeroth, seam_l[j].start)
 
     def pick(row, a, b):
         return jnp.where(assign[(5 * c + row // 64) // 2, p] == 0, a, b)
@@ -236,7 +242,7 @@
             d.wait_recv()
         a, b = square(gd[0]), square(gd[1])
         pack(lp.at[first], jnp.concatenate([pick(i, a[i:i + 64], b[i:i + 64]) for i in range(0, 320, 64)], axis=0))
-        for d in hg + [hh, ca]:
+        for d in both(hg, hh) + [ca]:
             d.start()
 
     @pl.when(off_home & plane1)
@@ -258,17 +264,19 @@
                         [pick(lo, a[:, 0:64], b[:, 0:64]), pick(160 + lo, a[:, 64:128], b[:, 64:128])], axis=1
                     )
             hg[j].start()
-        hh.start()
+            hh[j].start()
         ca.start()
 
     on(guest | off_home, sx.wait_recv, sc1.start)
 
     for j in range(NL):
         on(guest, hg[j].wait_recv)
-        on(guest & (plane1 | ~first_off), gg[j].start)
+        if j < len(gg):
+            on(guest & (plane1 | ~first_off), gg[j].start)
+    on(relay & late, *starts(zo))
     on(guest, ca.start)
-    on(guest & plane0 & first_off, *arrives(gg), cb.start)
-    on(off_home & plane0, hh.wait_recv, cb.start)
+    on(home & (plane1 | first_off), *arrives(hh[3:]), *starts(hf), *arrives(hh[:3]), cb.start)
+    on(guest & plane0 & first_off, *arrives(gg + hf), cb.start)
 
     for j in range(NZ):
         on(guest & plane0 & holds_diag, zd[j].wait_recv)
@@ -277,9 +285,27 @@
         on(guest & plane1 & holds_diag, zd[j].wait_recv, gs0[j].start)
     for j in range(NR):
         on(landing, zo[j].wait_recv)
-        on(landing & (plane1 | (p < MERGES - 1)), *starts(spread[0][j]))
-        on(landing & plane0 & (p > 0), *starts(spread[1][j]))
-    on(home & plane1, hh.wait_recv, cb.start)
+        on(landing & plane1, *starts(spread[j]))
+        on(landing & plane0 & (p < MERGES - 1), nr[j].start)
+        on(landing & plane0 & (p > 0), nl[j].start)
+
+    @pl.when(landing & plane0)
+    def _():
+        lanes = lax.broadcasted_iota(jnp.int32, (16, BLK), 1)
+        for j in range(NR):
+            nr[j].wait_recv()
+            nl[j].wait_recv()
+            for g in range(step // 16):
+                row = begin + j * step + g * 16
+                slab, t = row // TILE, row % TILE
+                low = assign[(5 + t // 64) // 2, p]
+                up = assign[(5 + (t + 160 * (slab // 2)) // 64) // 2, p]
+                at = pl.ds(j * step + g * 16, 16)
+                a, b = zn[0, at], zn[1, at]
+                zs[0, at] = jnp.where(jnp.where(lanes < 64, low, up) == 0, a, b)
+                zs[1, at] = jnp.where(assign[slab, p] == 0, a, b)
+            for d in chosen_spread[j]:
+                d.start()
 
     sc0.wait_recv()
     on(guest | diag_home, sc1.wait_recv)
@@ -369,12 +395,10 @@
 
     on(guest & plane0 & holds_diag, *[a for j in range(NZ) for a in (fr[j].wait_recv, gs0[j].start, fl[j].wait_recv, gs1[j].start)])
     for n in range(2):
-        on(guest & ~holds_diag, *arrives(came[0][n]), os0[n].start)
-        on(guest & plane0 & ~holds_diag, *arrives(came[1][n]), os1[n].start)
+        on(guest & ~holds_diag, *arrives(came[n]), os0[n].start)
     on(guest & ~holds_diag, *arrives(gs0))
     on(guest & ~holds_diag & plane0, *arrives(gs1))
     on(guest & holds_diag, *arrives(os0))
-    on(guest & holds_diag & plane0, *arrives(os1))
 
     def chosen(r, unpack, ref):
         a, b = unpack(ref[0]), unpack(ref[1])
@@ -389,11 +413,11 @@
         @pl.when(u == 2)
         def _():
             right(0, chosen(0, square, gd))
-            right(1, chosen(1, oblong, go))
+            right(1, oblong(go[0]))
 
         @pl.when(u == 3)
         def _():
-            right(0, chosen(0, flipped, go))
+            right(0, flipped(go[0]))
             right(1, chosen(1, square, gd))
 
         store_deviation(dot3(wh[0:320], wl[0:320], gh[...], gl[...]))
@@ -412,7 +436,7 @@
             right(1, square(gd[0]))
 
         values_times_right()
-        for d in gg:
+        for d in gg + hf:
             d.wait_recv()
         cb.start()
         ca.wait_recv()
@@ -439,7 +463,8 @@
     on(guest | diag_home, sx.wait_send)
     on(guest | off_home, sc1.wait_send)
     on(plane1 | first_off, cb.wait_send)
-    on(home & (plane1 | ~first_off), hh.wait_send)
+    on(home & (plane1 | ~first_off), *leaves(hh))
+    on(home & (plane1 | first_off), *leaves(hf))
     on(home, *leaves(hg))
     on(guest & (plane1 | ~first_off), *leaves(gg))
     on(diag_home, *leaves(zd))
@@ -451,12 +476,13 @@
     on(off_home & plane1, *leaves(yr + yl))
     on(off_home & (u == 0), *leaves(r0 + r1))
     on(relay, *leaves(zo))
-    on(relay & last, *leaves(flat(across[0])))
-    on(relay & zeroth, *leaves(flat(across[1])))
-    on(landing & (plane1 | (p < MERGES - 1)), *leaves(flat(spread[0])))
-    on(landing & plane0 & (p > 0), *leaves(flat(spread[1])))
+    on(relay & last, *leaves(seam_r))
+    on(relay & zeroth, *leaves(seam_l))
+    on(landing & plane1, *leaves(flat(spread)))
+    on(landing & plane0, *leaves(flat(chosen_spread)))
+    on(landing & plane0 & (p < MERGES - 1), *leaves(nr))
+    on(landing & plane0 & (p > 0), *leaves(nl))
     on(guest & ~holds_diag, *leaves(os0))
-    on(guest & ~holds_diag & plane0, *leaves(os1))
     on(guest & holds_diag, *leaves(gs0))
     on(guest & holds_diag & plane0, *leaves(gs1))
 
@@ -476,7 +502,7 @@
         out_specs=(vm, vm),
         scratch_shapes=[
             vmem(4, OFFD, BLK), vmem(4, OFFD, BLK), vmem(3, DIAG, BLK), vmem(2, OFFD, BLK),
-            vmem(TILE, TILE), vmem(TILE, TILE), vmem(OFFD, BLK), vmem(PART, BLK),
+            vmem(TILE, TILE), vmem(TILE, TILE), vmem(OFFD, BLK), vmem(PART, BLK), vmem(2, PART, BLK), vmem(2, PART, BLK),
         ]
         + [half(HALF)] * 8
         + [half(TILE)] * 6
@@ -486,7 +512,7 @@
             pltpu.SemaphoreType.DMA((160,)),
         ],
         compiler_params=pltpu.CompilerParams(
-            collective_id=0, has_side_effects=True, vmem_limit_bytes=48 << 20
+            collective_id=0, has_side_effects=True, vmem_limit_bytes=62 << 20
         ),
         name="refine",
     )(band_start, assignment.T, s, k)

time: 62.2 us -> 57.6 us (0.926)
  the two profiles are of different devices: /device:TPU:258 before, /device:TPU:37 now
where the time goes in v4:
time: 57.6 us; the launch traced here: 57.4 us
  Pallas kernels  54 us (94%)
  local copies, waits for them, and re-layouts  2.68 us (5%)
  between operations  0.65 us (1%)
    pallas_call x1, Pallas kernels, on_device(): pl.pallas_call(refine_kernel, out_shape=(shape, shape), in_specs=[sm, sm,...  54 us
    unnamed x4, local copies, waits for them, and re-layouts  2.68 us

profile of v4, /device:TPU:37, one launch (start us, length us, event | category | flops | bytes accessed | tf_op | source)
XLA Modules:
  0.0 57.4 jit_solution(7759111197619407712)
XLA Ops:
  0.6 54.0 %refine.1 = (f32[320,320]{1,0:T(8,128)}, f32[320,320]{1,0:T(8,128)}) custom-call(s32[10]{0:T(128)} %band.1, s32[5,32]{1,0:T(8,128)} %bitcast.9, f32[320,320]{1,0:T(8,128)} %bitcast.5, f32[320,320]{1,0:T(8,128)} %bitcast.6), custom_call_target="tpu_custom_call" | custom-call | tf_op jit(solution)/shard_map/refine/pallas_call | solution.py:498
  54.7 0.0 copy-start
  54.7 1.9 %copy.8 = f32[1,320,320]{2,1,0:T(8,128)} copy(f32[1,320,320]{2,1,0:T(8,128)} %bitcast.8) | data formatting | bytes 819200
  56.6 0.0 copy-done
  56.6 0.8 %copy.9 = f32[1,320,320]{2,1,0:T(8,128)} copy(f32[1,320,320]{2,1,0:T(8,128)S(1)} %bitcast.7) | data formatting | bytes 819200
Async XLA Ops:
  54.7 1.9 %copy-start = (f32[320,320]{1,0:T(8,128)S(1)}, f32[320,320]{1,0:T(8,128)}, u32[]{:S(2)}) copy-start(f32[320,320]{1,0:T(8,128)} %get-tuple-element.5) | copy-start | bytes 1228804

commit v5 on v4

--- a/solution.py
+++ b/solution.py
@@ -9,7 +9,7 @@
 BAND = 8
 TILE = 320
 HALF = 640
-DIAG = 576
+DIAG = 456
 OFFD = 800
 PART = 400
 MERGES = 32
@@ -55,11 +55,29 @@
     return oblong(v).T
 
 
+def ranks():
+    return lax.broadcasted_iota(jnp.int32, (BLK, BLK), 0), lax.broadcasted_iota(jnp.int32, (BLK, BLK), 1)
+
+
+def fold(ref, k):
+    i, j = ranks()
+    second = k[128:256, 128:256]
+    ref[0:128] = jnp.where(i >= j, k[0:128, 0:128], second)
+    ref[128:320] = k[128:320, 0:128]
+    ref[320:384] = k[256:320, 128:256]
+    ref[384:448] = jnp.concatenate([k[256:320, 256:320], jnp.zeros((64, 64), F32)], axis=1)
+    ref[448:456] = jnp.broadcast_to(jnp.sum(jnp.where(i == j, second, 0.0), axis=0, keepdims=True), (8, BLK))
+
+
 def square(v):
-    a, b, e = v[0:320], v[320:512], v[512:576, 0:64]
-    r0 = jnp.concatenate([a[0:128], a[128:320].T], axis=1)
-    r1 = jnp.concatenate([a[128:256], b[0:128], b[128:192].T], axis=1)
-    r2 = jnp.concatenate([a[256:320], b[128:192], e], axis=1)
+    i, j = ranks()
+    m, a, b, e, d = v[0:128], v[128:320], v[320:384], v[384:448, 0:64], v[448:449]
+    mt = m.T
+    d0 = jnp.where(i >= j, m, mt)
+    d1 = jnp.where(i < j, m, jnp.where(i > j, mt, d))
+    r0 = jnp.concatenate([d0, a.T], axis=1)
+    r1 = jnp.concatenate([a[0:128], d1, b.T], axis=1)
+    r2 = jnp.concatenate([a[128:192], b, e], axis=1)
     return jnp.concatenate([r0, r1, r2], axis=0)
 
 
@@ -133,10 +151,7 @@
 
     @pl.when(diag_home)
     def _():
-        gd[2, 0:320] = k[:, 0:128]
-        gd[2, 320:512] = k[128:320, 128:256]
-        gd[2, 512:576, 0:64] = k[256:320, 256:320]
-        gd[2, 512:576, 64:128] = jnp.zeros((64, 64), F32)
+        fold(gd.at[2], k)
 
     @pl.when(off_home)
     def _():
@@ -149,7 +164,7 @@
     load_s.wait()
     pack(sp.at[own_s], s)
 
-    NZ, NR, NL = 4, 5, 5
+    NZ, NR, NL = 3, 5, 5
     step = PART // NR
     twin = device(p, 1 - h, c, (u + 2) % 4)
     r0 = copies(ko.at[pl.ds(0, PART)], zb, PART, NR, device(p, h, c, 3))
@@ -487,6 +502,11 @@
     on(guest & holds_diag & plane0, *leaves(gs1))
 
 
+def hand_over_kernel(a, b, a_out, b_out):
+    a_out[...] = a[...]
+    b_out[...] = b[...]
+
+
 def on_device(intersection, children, band_start, assignment):
     s, k = intersection[0], children[0]
     vm = pl.BlockSpec(memory_space=pltpu.VMEM)
@@ -516,6 +536,14 @@
         ),
         name="refine",
     )(band_start, assignment.T, s, k)
+    refined, deviation = pl.pallas_call(
+        hand_over_kernel,
+        out_shape=(shape, shape),
+        in_specs=[vm, vm],
+        out_specs=(vm, vm),
+        compiler_params=pltpu.CompilerParams(vmem_limit_bytes=62 << 20),
+        name="hand_over",
+    )(refined, deviation)
     return refined[None], deviation[None]
 
 

time: 57.6 us -> 54.8 us (0.951)
  the two profiles are of different devices: /device:TPU:37 before, /device:TPU:4 now
where the time goes in v5:
time: 54.8 us; the launch traced here: 54.6 us
  Pallas kernels  53.9 us (98%)
  between operations  0.64 us (1%)
    pallas_call x1, Pallas kernels, on_device(): pl.pallas_call(refine_kernel, out_shape=(shape, shape), in_specs=[sm, sm,...  51.8 us
    pallas_call x1, Pallas kernels, on_device(): pl.pallas_call(hand_over_kernel, out_shape=(shape, shape), in_specs=[vm,...  2.15 us

profile of v5, /device:TPU:4, one launch (start us, length us, event | category | flops | bytes accessed | tf_op | source)
XLA Modules:
  0.0 54.6 jit_solution(340857714964343909)
XLA Ops:
  0.6 51.8 %refine.1 = (f32[320,320]{1,0:T(8,128)}, f32[320,320]{1,0:T(8,128)}) custom-call(s32[10]{0:T(128)} %band.1, s32[5,32]{1,0:T(8,128)} %bitcast.7, f32[320,320]{1,0:T(8,128)} %bitcast.5, f32[320,320]{1,0:T(8,128)} %bitcast.6), custom_call_target="tpu_custom_call" | custom-call | tf_op jit(solution)/shard_map/refine/pallas_call | solution.py:518
  52.4 2.2 %hand_over.1 = (f32[320,320]{1,0:T(8,128)}, f32[320,320]{1,0:T(8,128)}) custom-call(f32[320,320]{1,0:T(8,128)} %get-tuple-element.6.a, f32[320,320]{1,0:T(8,128)} %get-tuple-element.7.b), custom_call_target="tpu_custom_call" | custom-call | tf_op jit(solution)/shard_map/hand_over/pallas_call | solution.py:539

commit v6 on v5

--- a/solution.py
+++ b/solution.py
@@ -286,9 +286,9 @@
 
     for j in range(NL):
         on(guest, hg[j].wait_recv)
+        on(relay & late, zo[j].start)
         if j < len(gg):
             on(guest & (plane1 | ~first_off), gg[j].start)
-    on(relay & late, *starts(zo))
     on(guest, ca.start)
     on(home & (plane1 | first_off), *arrives(hh[3:]), *starts(hf), *arrives(hh[:3]), cb.start)
     on(guest & plane0 & first_off, *arrives(gg + hf), cb.start)
@@ -402,15 +402,18 @@
             rows = pl.ds(pl.multiple_of(i * 128, 128), 128)
             th[rows], tl[rows] = split(dot3(lh[rows], ll[rows], sh[...], sl[...]))
 
+    on(guest & plane0 & holds_diag, *[a for j in range(NZ) for a in (fr[j].wait_recv, gs0[j].start, fl[j].wait_recv, gs1[j].start)])
+    for n in range(2):
+        on(guest & ~holds_diag, *arrives(came[n]), os0[n].start)
+
+    @pl.when(guest & plane0)
+    def _():
         wh[0:320], wl[0:320] = th[own_rows], tl[own_rows]
         for i in range(2):
             rows = pl.ds(pl.multiple_of(TILE * c + 160 * i, 32), 160)
             at = pl.ds(320 + 160 * i, 160)
             wh[at], wl[at] = split(dot3(lh[rows], ll[rows], th[...], tl[...]))
 
-    on(guest & plane0 & holds_diag, *[a for j in range(NZ) for a in (fr[j].wait_recv, gs0[j].start, fl[j].wait_recv, gs1[j].start)])
-    for n in range(2):
-        on(guest & ~holds_diag, *arrives(came[n]), os0[n].start)
     on(guest & ~holds_diag, *arrives(gs0))
     on(guest & ~holds_diag & plane0, *arrives(gs1))
     on(guest & holds_diag, *arrives(os0))

time: 54.8 us -> 54.5 us (level)
  the two profiles are of different devices: /device:TPU:4 before, /device:TPU:7 now
where the time goes in v6:
time: 54.5 us; the launch traced here: 54.3 us
  Pallas kernels  53.7 us (99%)
  between operations  0.64 us (1%)
    pallas_call x1, Pallas kernels, on_device(): pl.pallas_call(refine_kernel, out_shape=(shape, shape), in_specs=[sm, sm,...  51.5 us
    pallas_call x1, Pallas kernels, on_device(): pl.pallas_call(hand_over_kernel, out_shape=(shape, shape), in_specs=[vm,...  2.15 us

profile of v6, /device:TPU:7, one launch (start us, length us, event | category | flops | bytes accessed | tf_op | source)
XLA Modules:
  0.0 54.3 jit_solution(7640859713250296550)
XLA Ops:
  0.6 51.5 %refine.1 = (f32[320,320]{1,0:T(8,128)}, f32[320,320]{1,0:T(8,128)}) custom-call(s32[10]{0:T(128)} %band.1, s32[5,32]{1,0:T(8,128)} %bitcast.7, f32[320,320]{1,0:T(8,128)} %bitcast.5, f32[320,320]{1,0:T(8,128)} %bitcast.6), custom_call_target="tpu_custom_call" | custom-call | tf_op jit(solution)/shard_map/refine/pallas_call | solution.py:521
  52.2 2.2 %hand_over.1 = (f32[320,320]{1,0:T(8,128)}, f32[320,320]{1,0:T(8,128)}) custom-call(f32[320,320]{1,0:T(8,128)} %get-tuple-element.6.a, f32[320,320]{1,0:T(8,128)} %get-tuple-element.7.b), custom_call_target="tpu_custom_call" | custom-call | tf_op jit(solution)/shard_map/hand_over/pallas_call | solution.py:542

commit v7 on v6

--- a/solution.py
+++ b/solution.py
@@ -36,8 +36,10 @@
 
 
 def dot3(ah, al, bh, bl):
+    n = ah.shape[0]
     d = lambda a, b: jnp.dot(a, b, preferred_element_type=F32)
-    return d(ah, bh) + (d(ah, bl) + d(al, bh))
+    both = d(jnp.concatenate([ah, al], axis=0), bh)
+    return both[:n] + (d(ah, bl) + both[n:])
 
 
 def pack(ref, v):
@@ -228,11 +230,11 @@
 
     pl.semaphore_wait(barrier, len(friends) + 8 * seam.astype(jnp.int32))
 
+    on(diag_home & last, *starts(sr))
+    on(diag_home & zeroth, *starts(sw))
     on(off_home & (u == 0), *starts(both(r0, r1)))
     y = p % 4
     on(diag_home & plane1, *starts(both(fr, fl)))
-    on(diag_home & last, *starts(sr))
-    on(diag_home & zeroth, *starts(sw))
     on(diag_home, *starts(zd))
     on(off_home & plane1, *starts(both(yr, yl)))
     on(home & plane0, *starts(hg), ca.start)
@@ -244,9 +246,9 @@
     for j in range(NR):
         on(relay & (u == 3), r0[j].wait_recv)
         on(relay & (u == 2), r1[j].wait_recv)
-        on(relay & ~late, zo[j].start)
         on(relay & last, seam_r[j].start)
         on(relay & zeroth, seam_l[j].start)
+        on(relay & ~late, zo[j].start)
 
     def pick(row, a, b):
         return jnp.where(assign[(5 * c + row // 64) // 2, p] == 0, a, b)

time: 54.5 us -> 54.3 us (level)
  no operation moved by 1% of the time
where the time goes in v7:
time: 54.3 us; the launch traced here: 54.1 us
  Pallas kernels  53.5 us (99%)
  between operations  0.64 us (1%)
    pallas_call x1, Pallas kernels, on_device(): pl.pallas_call(refine_kernel, out_shape=(shape, shape), in_specs=[sm, sm,...  51.3 us
    pallas_call x1, Pallas kernels, on_device(): pl.pallas_call(hand_over_kernel, out_shape=(shape, shape), in_specs=[vm,...  2.15 us

profile of v7, /device:TPU:7, one launch (start us, length us, event | category | flops | bytes accessed | tf_op | source)
XLA Modules:
  0.0 54.1 jit_solution(6072874207533072075)
XLA Ops:
  0.6 51.3 %refine.1 = (f32[320,320]{1,0:T(8,128)}, f32[320,320]{1,0:T(8,128)}) custom-call(s32[10]{0:T(128)} %band.1, s32[5,32]{1,0:T(8,128)} %bitcast.7, f32[320,320]{1,0:T(8,128)} %bitcast.5, f32[320,320]{1,0:T(8,128)} %bitcast.6), custom_call_target="tpu_custom_call" | custom-call | tf_op jit(solution)/shard_map/refine/pallas_call | solution.py:523
  51.9 2.2 %hand_over.1 = (f32[320,320]{1,0:T(8,128)}, f32[320,320]{1,0:T(8,128)}) custom-call(f32[320,320]{1,0:T(8,128)} %get-tuple-element.6.a, f32[320,320]{1,0:T(8,128)} %get-tuple-element.7.b), custom_call_target="tpu_custom_call" | custom-call | tf_op jit(solution)/shard_map/hand_over/pallas_call | solution.py:544
